TPU v7x, 32 devices: a whole 2x2x4 slice. The times are simulated.
32 devices in a mesh: seg: 4 (over x, core), sec: 8 (over z, y).
Axes of the slice: x: 2, y: 2, z: 4, core: 2. Of those that a mesh axis runs over, the one named last changes fastest.
Arguments:
- left_environment: bfloat16 [4, 64, 64, 1920], P('seg', 'sec'), may hold values from -0.125 to 0.125
- right_environment: bfloat16 [4, 64, 64, 1920], P('seg', 'sec'), may hold values from -0.75 to 0.75
- site_previous: bfloat16 [4, 64, 64, 256], P('seg', 'sec'), may hold values from -0.75 to 0.75
- state_start: float32 [4, 64, 64, 256], P('seg', 'sec'), may hold values from -36 to 36
- preconditioner: float32 [4, 64, 64, 256], P('seg', 'sec'), may hold values from 0.25 to 4
- channel_tensor: bfloat16 [30, 4, 30, 4], replicated, may hold values from -0.5 to 0.5
- channel_mask: int32 [30, 30], replicated, may hold values 0 or 1
- sector_shift: int32 [5, 64], replicated, may hold values from 0 to 63, as said below
- left_sizes: int32 [64], replicated, may hold values from 32 to 64, as said below
- right_sizes: int32 [64, 4], replicated, may hold values from 32 to 64, as said below
Outputs:
- bond_state: float32 [4, 64, 64, 256], P('seg', 'sec')
- energy: float32 [4], P('seg')
Inputs may be any that keep to these rules, and one draw needn't show every extreme that they name: Each row is a permutation of the 64 sectors; for every group of 8 consecutive sectors and every other such group, at most 5 pairs of a class k and a sector l of the first group have sector_shift[k, l] in the second group, and some pair of groups reaches 5. `left_sizes`: some sector fills its tile and some has 32 live states. `right_sizes`: some block fills its tile and some has 32 live states.
All inputs are finite; a program needn't handle non-finite values.
Results may differ from a plain program's by a relative error of at most 0.012.
Values may be sent and summed in bfloat16 or wider, within the bound.
A program may use at most 256 MiB of HBM per device.

v0:
```python
import jax
import jax.numpy as jnp
from jax import lax
from jax.sharding import PartitionSpec as P

W = 30
D = 4
B = 64
SEC_DEV = 8
CLASSES = 5
ITERS = 2


EPSILON = 1e-06
HIGHEST_PRECISION = lax.Precision.HIGHEST


def passed_along(block, axis, distance):
    devices = range(lax.axis_size(axis))
    route = [(i - distance, i) for i in devices if i - distance in devices]
    return lax.ppermute(block, axis, route)


def live_masks(left_sizes, right_sizes, offset):
    row_limit = lax.dynamic_slice_in_dim(left_sizes, offset, SEC_DEV, 0)
    column_limit = lax.dynamic_slice_in_dim(right_sizes, offset, SEC_DEV, 0)
    row_live = jnp.arange(B, dtype=jnp.int32)[None, :] < row_limit[:, None]
    column_live = jnp.arange(B, dtype=jnp.int32)[None, None, :] < column_limit[:, :, None]
    joined_live = row_live[:, :, None, None] & column_live[:, None, :, :]
    return joined_live.astype(jnp.float32).reshape(SEC_DEV, B, D * B)


def pair_layout(sector_shift, group):
    target_list = lax.dynamic_slice_in_dim(sector_shift, group * SEC_DEV, SEC_DEV, 1).T.reshape(
        SEC_DEV * CLASSES
    )
    owner_list = target_list // SEC_DEV
    order = jnp.arange(SEC_DEV * CLASSES, dtype=jnp.int32)
    earlier = order[None, :] < order[:, None]
    same_target = target_list[:, None] == target_list[None, :]
    leading = jnp.logical_not(jnp.any(same_target & earlier, axis=1))
    rank_list = jnp.sum(
        ((owner_list[:, None] == owner_list[None, :]) & earlier).astype(jnp.int32), axis=1
    )
    return (target_list, owner_list, leading, rank_list, same_target)


def build_environment(environment, site_blocks, channel_mix, sector_shift, offset):
    every_site = lax.all_gather(site_blocks, "sec", axis=0, tiled=True)
    groups = W // CLASSES
    split_left = environment.reshape(SEC_DEV, B, CLASSES, groups, B)
    own_tensor = site_blocks.reshape(SEC_DEV, B, D, B)
    every_tensor = every_site.reshape(every_site.shape[0], B, D, B)
    contracted = jnp.einsum(
        "lpkja,lasb->lpkjsb", split_left, own_tensor, preferred_element_type=jnp.float32
    ).astype(jnp.bfloat16)
    channel_split = channel_mix.reshape(CLASSES, groups, D, W, D)
    accumulated = jnp.zeros((SEC_DEV, B, W, B), jnp.float32)
    for charge in range(CLASSES):
        targets = lax.dynamic_slice_in_dim(sector_shift[charge], offset, SEC_DEV, 0)
        shifted_site = jnp.take(every_tensor, targets, axis=0)
        carried = jnp.einsum(
            "jtvs,lpjsb->lptvb",
            channel_split[charge],
            contracted[:, :, charge],
            preferred_element_type=jnp.float32,
        ).astype(jnp.bfloat16)
        accumulated = accumulated + jnp.einsum(
            "lpte,lptvb->levb", shifted_site, carried, preferred_element_type=jnp.float32
        )
    return accumulated.astype(jnp.bfloat16).reshape(SEC_DEV, B, W * B)


def apply_operator(vector_low, left_split, right_split, channel_mix, routing, live_mask):
    blocks = vector_low.reshape(SEC_DEV, B, D, B)
    right_product = jnp.einsum(
        "lasb,lbvc->lasvc", blocks, right_split, preferred_element_type=jnp.float32
    ).astype(jnp.bfloat16)
    mixed_product = jnp.einsum(
        "wtvs,lasvc->lwatc", channel_mix, right_product, preferred_element_type=jnp.float32
    ).astype(jnp.bfloat16)
    grouped = mixed_product.reshape(SEC_DEV, CLASSES, W // CLASSES, B, D, B)
    partial_value = jnp.einsum(
        "lpkja,lkjatc->lkptc", left_split, grouped, preferred_element_type=jnp.float32
    )
    partial_value = partial_value.reshape(SEC_DEV * CLASSES, B * D * B)
    onehot, send_matrix, take_matrix = routing
    outgoing = jnp.dot(
        send_matrix, partial_value, precision=HIGHEST_PRECISION, preferred_element_type=jnp.float32
    ).astype(jnp.bfloat16)
    outgoing = outgoing.reshape(lax.axis_size("sec"), -1, B * D * B)
    arrived = lax.all_to_all(outgoing, "sec", split_axis=0, concat_axis=0, tiled=True)
    summed = jnp.dot(
        take_matrix, arrived.reshape(-1, B * D * B), preferred_element_type=jnp.float32
    )
    return live_mask * summed.reshape(SEC_DEV, B, D * B)


def on_device(
    left_environment,
    right_environment,
    site_previous,
    state_start,
    preconditioner,
    channel_tensor,
    channel_mask,
    sector_shift,
    left_sizes,
    right_sizes,
):
    group_total = lax.axis_size("sec")
    my_group = lax.axis_index("sec")
    offset = my_group * SEC_DEV
    sectors = SEC_DEV * group_total
    capacity = (CLASSES * SEC_DEV + group_total - 1) // group_total
    channel_mix = channel_tensor * channel_mask.astype(jnp.bfloat16)[:, None, :, None]
    live_mask = live_masks(left_sizes, right_sizes, offset)
    own_left = left_environment[0]
    fresh = build_environment(own_left, site_previous[0], channel_mix, sector_shift, offset)
    handed = passed_along(fresh, "seg", 1)
    position = lax.axis_index("seg")
    left_used = jnp.where(position == 0, own_left, handed)
    came_right = passed_along(right_environment[0], "seg", -1)
    right_used = jnp.where(position == lax.axis_size("seg") - 1, right_environment[0], came_right)
    left_split = left_used.reshape(SEC_DEV, B, CLASSES, W // CLASSES, B)
    right_split = right_used.reshape(SEC_DEV, B, W, B)
    target_list, owner_list, leading, rank_list, same_target = pair_layout(sector_shift, my_group)
    onehot = (jnp.arange(sectors, dtype=jnp.int32)[:, None] == target_list[None, :]).astype(
        jnp.float32
    )
    merge_matrix = (leading[:, None] & same_target).astype(jnp.float32)
    slot_owner = jnp.repeat(jnp.arange(group_total, dtype=jnp.int32), capacity)
    slot_rank = jnp.tile(jnp.arange(capacity, dtype=jnp.int32), group_total)
    slot_matrix = (
        (owner_list[None, :] == slot_owner[:, None]) & (rank_list[None, :] == slot_rank[:, None])
    ).astype(jnp.float32)
    send_matrix = jnp.dot(
        slot_matrix, merge_matrix, precision=HIGHEST_PRECISION, preferred_element_type=jnp.float32
    )
    every_target, every_owner, every_leading, every_rank, unused_same = jax.vmap(
        lambda group: pair_layout(sector_shift, group)
    )(jnp.arange(group_total, dtype=jnp.int32))
    local_target = every_target - offset
    hits = (every_owner == my_group) & every_leading
    take_table = (
        hits[:, None, None, :]
        & (
            every_rank[:, None, None, :]
            == jnp.arange(capacity, dtype=jnp.int32)[None, None, :, None]
        )
        & (
            local_target[:, None, None, :]
            == jnp.arange(SEC_DEV, dtype=jnp.int32)[None, :, None, None]
        )
    )
    take_matrix = jnp.sum(take_table.astype(jnp.float32), axis=3)
    take_matrix = (
        jnp.transpose(take_matrix, (1, 0, 2))
        .reshape(SEC_DEV, group_total * capacity)
        .astype(jnp.bfloat16)
    )
    routing = (onehot, send_matrix, take_matrix)
    total_entries = float(SEC_DEV * B * D * B * group_total)

    def operator(vector):
        return apply_operator(
            vector.astype(jnp.bfloat16), left_split, right_split, channel_mix, routing, live_mask
        )

    def rayleigh(vector, result):
        return lax.psum(jnp.sum(vector * result), "sec") / total_entries

    current = live_mask * state_start[0]
    start_square = lax.psum(jnp.sum(current * current), "sec") / total_entries
    current = current / jnp.sqrt(start_square + EPSILON)
    applied = operator(current)
    precondition = preconditioner[0]
    for iteration in range(ITERS):
        rayleigh_value = rayleigh(current, applied)
        correction = precondition * (applied - rayleigh_value * current)
        correlation_value = lax.psum(jnp.sum(current * correction), "sec") / total_entries
        correction = correction - correlation_value * current
        squared_length = lax.psum(jnp.sum(correction * correction), "sec") / total_entries
        direction = correction / jnp.sqrt(squared_length + EPSILON)
        product = operator(direction)
        sums = lax.psum(
            (
                jnp.sum(current * product),
                jnp.sum(direction * applied),
                jnp.sum(direction * product),
            ),
            "sec",
        )
        cross_term = 0.5 * (sums[0] + sums[1]) / total_entries
        far_term = sums[2] / total_entries
        rotation = 0.5 * jnp.arctan2(-2.0 * cross_term, far_term - rayleigh_value)
        cosine = jnp.cos(rotation)
        sine = jnp.sin(rotation)
        current = cosine * current + sine * direction
        applied = cosine * applied + sine * product
    energy_value = rayleigh(current, applied)
    return (current[None], jnp.reshape(energy_value, (1,)))


def solution(mesh):
    in_specs = (
        P("seg", "sec", None, None),
        P("seg", "sec", None, None),
        P("seg", "sec", None, None),
        P("seg", "sec", None, None),
        P("seg", "sec", None, None),
        P(),
        P(),
        P(),
        P(),
        P(),
    )
    out_specs = (P("seg", "sec", None, None), P("seg"))
    return jax.shard_map(
        on_device, mesh=mesh, in_specs=in_specs, out_specs=out_specs, check_vma=False
    )
```

profile of v0, /device:TPU:0, one launch (start us, length us, event | category | flops | bytes accessed | tf_op | source)
XLA Modules:
  0.0 942.3 jit_solution(4993979414029227872)
XLA Ops:
  14.5 6.9 reshape_squeeze.6
  21.4 10.1 %convolution_convert_fusion.3 = bf16[8,64,5,6,4,64]{5,1,4,3,2,0:T(8,128)(2,1)} fusion(bf16[8,64,5,6,64,1]{4,3,2,1,0,5:T(8,128)(2,1)} %bitcast.331, bf16[8,64,4,64,1,1]{3,2,1,0,5,4:T(4,128)(2,1)S(1)} %bitcast.340), kind=kOutput, calls=%fused_computation.51 | convolution fusion | flops 507248640 | bytes 10092544 | tf_op jit(solution)/shard_map/lpkja,lasb->lpkjsb/dot_general | solution.py:54
  31.5 11.2 %slice_bitcast_fusion.4 = (bf16[8,64,6,4,64,1]{4,1,3,2,0,5:T(8,128)(2,1)S(1)}, bf16[8,64,6,4,64,1]{4,1,3,2,0,5:T(8,128)(2,1)S(1)}, bf16[8,64,6,4,64,1]{4,1,3,2,0...) fusion(bf16[8,64,5,6,4,64]{5,1,4,3,2,0:T(8,128)(2,1)} %convolution_convert_fusion.3), kind=kLoop, calls=%fused_computation.62 | loop fusion | bytes 15728640 | tf_op jit(solution)/shard_map/squeeze | solution.py:65
  43.3 8.9 fusion.4
  52.2 8.9 fusion.3
  62.4 9.1 fusion.2
  79.1 23.8 %psum.98 = f32[]{:T(128)} all-reduce(f32[]{:T(128)} %multiply_reduce_fusion.13), channel_id=1, replica_groups=mesh['seg'=4,'sec'=8] {'sec'}, use_global_device_ids=true, to_apply=%region_1.2 | all-reduce | flops 1 | bytes 8 | tf_op jit(solution)/shard_map/psum | solution.py:174
  105.5 10.6 %fusion.1 = bf16[8,64,4,30,64]{4,3,2,1,0:T(8,128)(2,1)} fusion(bf16[8,64,6,4,64,1]{4,1,3,2,0,5:T(8,128)(2,1)} %get-tuple-element.62, bf16[30,4,30,4]{2,3,0,1:T(4,128)(2,1)S(1)} %copy_multiply_fusion), kind=kOutput, calls=%fused_computation.19 | convolution fusion | flops 192675840 | bytes 9461760 | tf_op jit(solution)/shard_map/jtvs,lpjsb->lptvb/dot_general | solution.py:62
  116.1 9.0 fusion
  127.0 5.2 reshape.347
  132.3 7.1 reshape.344
  139.3 5.3 copy.185
  144.7 3.0 gather_fusion.4
  147.6 3.0 gather_fusion.3
  150.6 3.0 gather_fusion.2
  153.6 3.0 gather_fusion.1
  156.5 3.0 gather_fusion
  159.5 17.2 %fusion.20 = f32[8,64,30,64,1]{3,1,4,2,0:T(8,128)S(1)} fusion(bf16[8,64,4,30,64]{4,3,2,1,0:T(8,128)(2,1)} %fusion.4, bf16[8,64,4,64]{3,1,2,0:T(8,128)(2,1)S(1)} %gather_fusion.4, pred[8]{0:T(512)(128)(4,1)S(1)} %copy-done.27), kind=kOutput, calls=%fused_computation.38 | convolution fusion | flops 503447552 | bytes 12058632 | tf_op jit(solution)/shard_map/lpte,lptvb->levb/dot_general | solution.py:68
  176.8 18.2 %fusion.22 = f32[8,64,30,64,1]{3,1,4,2,0:T(8,128)} fusion(bf16[8,64,4,30,64]{4,3,2,1,0:T(8,128)(2,1)} %fusion.3, bf16[8,64,4,64]{3,1,2,0:T(8,128)(2,1)S(1)} %gather_fusion.3, pred[8]{0:T(512)(128)(4,1)S(1)} %copy-done.26), kind=kOutput, calls=%fused_computation.40 | convolution fusion | flops 503447552 | bytes 12058632 | tf_op jit(solution)/shard_map/lpte,lptvb->levb/dot_general | solution.py:68
  195.0 18.5 %fusion.24 = f32[8,64,30,64,1]{3,1,4,2,0:T(8,128)} fusion(bf16[8,64,4,30,64]{4,3,2,1,0:T(8,128)(2,1)} %fusion.2, bf16[8,64,4,64]{3,1,2,0:T(8,128)(2,1)S(1)} %gather_fusion.2, pred[8]{0:T(512)(128)(4,1)S(1)} %copy-done.29), kind=kOutput, calls=%fused_computation.42 | convolution fusion | flops 503447552 | bytes 12058632 | tf_op jit(solution)/shard_map/lpte,lptvb->levb/dot_general | solution.py:68
  213.5 18.6 %fusion.26 = f32[8,64,30,64,1]{3,1,4,2,0:T(8,128)} fusion(bf16[8,64,4,30,64]{4,3,2,1,0:T(8,128)(2,1)} %fusion.1, bf16[8,64,4,64]{3,1,2,0:T(8,128)(2,1)S(1)} %gather_fusion.1, pred[8]{0:T(512)(128)(4,1)S(1)} %copy-done.28), kind=kOutput, calls=%fused_computation.44 | convolution fusion | flops 503447552 | bytes 12058632 | tf_op jit(solution)/shard_map/lpte,lptvb->levb/dot_general | solution.py:68
  232.1 23.9 %fusion.36 = bf16[8,64,30,64]{3,1,2,0:T(8,128)(2,1)S(1)} fusion(f32[8,64,30,64,1]{3,1,4,2,0:T(8,128)S(1)} %fusion.20, f32[8,64,30,64,1]{3,1,4,2,0:T(8,128)} %fusion.22, f32[8,64,30,64,1]{3,1,4,2,0:T(8,128)} %fusion.24, f32[8,64,30,64,1]{3,1,4,2,0:T(8,128)} %fusion.26, bf16[8,64,4,30,64]{4,3,2,1,0:T(8,128)(2,1)} %fusion, ...), kind=kOutput, calls=%fused_computation.53 | convolution fusion | flops 508362752 | bytes 25821192 | tf_op jit(solution)/shard_map/lpte,lptvb->levb/dot_general | solution.py:68
  256.0 4.6 copy.208
  260.6 5.7 reshape.345
  268.9 10.3 %convert_bitcast_fusion.2 = bf16[8,64,4,30,64,1]{4,1,3,2,0,5:T(8,128)(2,1)} fusion(bf16[8,64,30,64,1]{3,2,1,0,4:T(8,128)(2,1)} %bitcast.328, f32[8,64,4,64]{3,2,1,0:T(4,128)S(1)} %copy-done.8, f32[]{:T(128)S(6)} %sqrt.9, pred[8,4,64]{2,1,0:T(4,128)(4,1)S(1)} %copy-done.23, pred[8,64]{1,0:T(8,128)(4,1)S(1)} %copy-done.24), kind=kOutput, calls=%fused_computation.50 | convolution fusion | flops 507772928 | bytes 10357252 | tf_op jit(solution)/shard_map/lasb,lbvc->lasvc/dot_general | solution.py:76
  279.2 46.9 %fusion.5 = bf16[8,30,64,4,64]{4,1,3,2,0:T(8,128)(2,1)} fusion(bf16[8,64,4,30,64,1]{4,1,3,2,0,5:T(8,128)(2,1)} %convert_bitcast_fusion.2, bf16[30,4,30,4,1,1]{2,3,0,1,5,4:T(4,128)(2,1)S(1)} %fusion.151), kind=kOutput, calls=%fused_computation.23 | convolution fusion | flops 947650560 | bytes 15757440 | tf_op jit(solution)/shard_map/wtvs,lasvc->lwatc/dot_general | solution.py:79
  326.1 18.4 %copy.215 = bf16[8,30,64,4,64]{4,2,3,1,0:T(8,128)(2,1)} copy(bf16[8,30,64,4,64]{4,1,3,2,0:T(8,128)(2,1)} %fusion.5) | data formatting | bytes 15728640 | tf_op jit(solution)/shard_map/convert_element_type | solution.py:81
  344.8 4.4 reshape.346
  349.2 12.5 %fusion.48 = f32[8,5,64,4,64]{4,2,3,1,0:T(8,128)} fusion(bf16[8,5,6,64,4,64]{5,3,4,2,1,0:T(8,128)(2,1)} %bitcast.332, bf16[8,64,5,6,64,1]{4,3,2,1,0,5:T(8,128)(2,1)} %bitcast.335), kind=kOutput, calls=%fused_computation.71 | convolution fusion | flops 503316480 | bytes 12451840 | tf_op jit(solution)/shard_map/lpkja,lkjatc->lkptc/dot_general | solution.py:83
  361.7 9.5 %copy.218 = f32[8,5,64,4,64]{4,3,2,1,0:T(4,128)} copy(f32[8,5,64,4,64]{4,2,3,1,0:T(8,128)} %fusion.48) | data formatting | bytes 5242880 | tf_op jit(solution)/shard_map/lpkja,lkjatc->lkptc/dot_general | solution.py:83
  371.2 5.4 reshape.349
  376.6 3.3 convolution_convert_fusion.2
  380.0 3.3 reshape.350
  383.3 3.7 all-to-all-start
  387.1 10.5 %while.1 = (s32[]{:T(128)}, s32[5,64]{1,0:T(8,128)S(1)}, s32[8,2]{0,1:T(2,128)S(1)}, s32[8,5,8]{2,1,0:T(8,128)S(1)}, s32[]{:T(128)}) while((s32[]{:T(128)}, s32[5,64]{1,0:T(8,128)S(1)}, s32[8,2]{0,1:T(2,128)S(1)}, s32[8,5,8]{2,1,0:T(8,128)S(1)}, s32[]{:T(128)}) %tuple.63), condition=%wide.while_cond, body=%wide.while_body.sunk | while | flops 2 | bytes 8289 | solution.py:34
  398.6 36.2 %all-to-all-done = bf16[8,5,16384]{2,1,0:T(8,128)(2,1)S(1)} async-done(((bf16[8,5,16384]{2,1,0:T(8,128)(2,1)}), bf16[8,5,16384]{2,1,0:T(8,128)(2,1)S(1)}, u32[]{:S(2)}, u32[]{:S(2)}) %all-to-all-start) | async-done | bytes 1310752 | tf_op jit(solution)/shard_map/all_to_all | solution.py:92
  438.9 21.8 %psum.99 = f32[]{:T(128)} all-reduce(f32[]{:T(128)} %get-tuple-element.70), channel_id=1, replica_groups=mesh['seg'=4,'sec'=8] {'sec'}, use_global_device_ids=true, to_apply=%region_8.10 | all-reduce | flops 1 | bytes 8 | tf_op jit(solution)/shard_map/psum | solution.py:171
  462.8 17.7 %psum.100 = f32[]{:T(128)} all-reduce(f32[]{:T(128)} %multiply_reduce_fusion.11), channel_id=1, replica_groups=mesh['seg'=4,'sec'=8] {'sec'}, use_global_device_ids=true, to_apply=%region_10.12 | all-reduce | flops 1 | bytes 8 | tf_op jit(solution)/shard_map/psum | solution.py:181
  482.5 19.8 %psum.101 = f32[]{:T(128)} all-reduce(f32[]{:T(128)} %get-tuple-element.44), channel_id=1, replica_groups=mesh['seg'=4,'sec'=8] {'sec'}, use_global_device_ids=true, to_apply=%region_12.14 | all-reduce | flops 1 | bytes 8 | tf_op jit(solution)/shard_map/psum | solution.py:183
  503.2 10.1 %convert_bitcast_fusion.1 = bf16[8,64,4,30,64,1]{4,1,3,2,0,5:T(8,128)(2,1)} fusion(bf16[8,64,30,64,1]{3,2,1,0,4:T(8,128)(2,1)} %bitcast.329, bf16[8,64,4,64,1]{3,2,0,1,4:T(4,128)(2,1)S(1)} %bitcast.339), kind=kOutput, calls=%fused_computation.49 | convolution fusion | flops 507248640 | bytes 10092544 | tf_op jit(solution)/shard_map/lasb,lbvc->lasvc/dot_general | solution.py:76
  513.3 46.9 %fusion.6 = bf16[8,30,64,4,64]{4,1,3,2,0:T(8,128)(2,1)} fusion(bf16[8,64,4,30,64,1]{4,1,3,2,0,5:T(8,128)(2,1)} %convert_bitcast_fusion.1, bf16[30,4,30,4,1,1]{2,3,0,1,5,4:T(4,128)(2,1)S(1)} %fusion.151), kind=kOutput, calls=%fused_computation.24 | convolution fusion | flops 947650560 | bytes 15757440 | tf_op jit(solution)/shard_map/wtvs,lasvc->lwatc/dot_general | solution.py:79
  560.2 18.2 %copy.224 = bf16[8,30,64,4,64]{4,2,3,1,0:T(8,128)(2,1)} copy(bf16[8,30,64,4,64]{4,1,3,2,0:T(8,128)(2,1)} %fusion.6) | data formatting | bytes 15728640 | tf_op jit(solution)/shard_map/convert_element_type | solution.py:81
  578.5 12.5 %fusion.51 = f32[8,5,64,4,64]{4,2,3,1,0:T(8,128)} fusion(bf16[8,5,6,64,4,64]{5,3,4,2,1,0:T(8,128)(2,1)} %bitcast.334, bf16[8,64,5,6,64,1]{4,3,2,1,0,5:T(8,128)(2,1)} %bitcast.336), kind=kOutput, calls=%fused_computation.72 | convolution fusion | flops 503316480 | bytes 12451840 | tf_op jit(solution)/shard_map/lpkja,lkjatc->lkptc/dot_general | solution.py:83
  590.9 9.5 %copy.227 = f32[8,5,64,4,64]{4,3,2,1,0:T(4,128)} copy(f32[8,5,64,4,64]{4,2,3,1,0:T(8,128)} %fusion.51) | data formatting | bytes 5242880 | tf_op jit(solution)/shard_map/lpkja,lkjatc->lkptc/dot_general | solution.py:83
  600.4 5.2 reshape.354
  605.6 3.3 convolution_convert_fusion.1
  611.0 40.6 %all_to_all.15 = bf16[8,5,16384]{2,1,0:T(8,128)(2,1)} all-to-all(bf16[8,5,16384]{2,1,0:T(8,128)(2,1)S(1)} %reshape.355), channel_id=1, replica_groups=mesh['seg'=4,'sec'=8] {'sec'}, dimensions={0} | all-to-all | bytes 2621440 | tf_op jit(solution)/shard_map/all_to_all | solution.py:92
  651.6 3.3 reshape.356
  654.9 3.6 multiply_reduce_fusion.7
  659.8 20.2 %all-reduce.2 = (f32[]{:T(128)}, f32[]{:T(128)}) all-reduce(f32[]{:T(128)S(6)} %add.122, f32[]{:T(128)} %get-tuple-element.24), channel_id=1, replica_groups=mesh['seg'=4,'sec'=8] {'sec'}, use_global_device_ids=true, to_apply=%region_14.16 | all-reduce | flops 2 | bytes 16 | tf_op jit(solution)/shard_map/psum | solution.py:186
  683.8 17.7 %psum.105 = f32[]{:T(128)} all-reduce(f32[]{:T(128)} %get-tuple-element.41), channel_id=1, replica_groups=mesh['seg'=4,'sec'=8] {'sec'}, use_global_device_ids=true, to_apply=%region_20.22 | all-reduce | flops 1 | bytes 8 | tf_op jit(solution)/shard_map/psum | solution.py:171
  703.1 19.7 %psum.106 = f32[]{:T(128)} all-reduce(f32[]{:T(128)} %multiply_reduce_fusion.5), channel_id=1, replica_groups=mesh['seg'=4,'sec'=8] {'sec'}, use_global_device_ids=true, to_apply=%region_22.24 | all-reduce | flops 1 | bytes 8 | tf_op jit(solution)/shard_map/psum | solution.py:181
  724.5 17.9 %psum.107 = f32[]{:T(128)} all-reduce(f32[]{:T(128)} %get-tuple-element.39), channel_id=1, replica_groups=mesh['seg'=4,'sec'=8] {'sec'}, use_global_device_ids=true, to_apply=%region_24.26 | all-reduce | flops 1 | bytes 8 | tf_op jit(solution)/shard_map/psum | solution.py:183
  743.4 10.1 %convert_bitcast_fusion = bf16[8,64,4,30,64,1]{4,1,3,2,0,5:T(8,128)(2,1)} fusion(bf16[8,64,30,64,1]{3,2,1,0,4:T(8,128)(2,1)} %bitcast.330, bf16[8,64,4,64,1]{3,2,0,1,4:T(4,128)(2,1)S(1)} %bitcast.338), kind=kOutput, calls=%fused_computation.48 | convolution fusion | flops 507248640 | bytes 10092544 | tf_op jit(solution)/shard_map/lasb,lbvc->lasvc/dot_general | solution.py:76
  753.5 46.9 %fusion.7 = bf16[8,30,64,4,64]{4,1,3,2,0:T(8,128)(2,1)} fusion(bf16[8,64,4,30,64,1]{4,1,3,2,0,5:T(8,128)(2,1)} %convert_bitcast_fusion, bf16[30,4,30,4,1,1]{2,3,0,1,5,4:T(4,128)(2,1)S(1)} %fusion.151), kind=kOutput, calls=%fused_computation.25 | convolution fusion | flops 947650560 | bytes 15757440 | tf_op jit(solution)/shard_map/wtvs,lasvc->lwatc/dot_general | solution.py:79
  800.4 18.0 %copy.233 = bf16[8,30,64,4,64]{4,2,3,1,0:T(8,128)(2,1)} copy(bf16[8,30,64,4,64]{4,1,3,2,0:T(8,128)(2,1)} %fusion.7) | data formatting | bytes 15728640 | tf_op jit(solution)/shard_map/convert_element_type | solution.py:81
  818.4 12.5 %fusion.54 = f32[8,5,64,4,64]{4,2,3,1,0:T(8,128)} fusion(bf16[8,5,6,64,4,64]{5,3,4,2,1,0:T(8,128)(2,1)} %bitcast.333, bf16[8,64,5,6,64,1]{4,3,2,1,0,5:T(8,128)(2,1)} %bitcast.337), kind=kOutput, calls=%fused_computation.73 | convolution fusion | flops 503316480 | bytes 12451840 | tf_op jit(solution)/shard_map/lpkja,lkjatc->lkptc/dot_general | solution.py:83
  830.9 9.5 %copy.236 = f32[8,5,64,4,64]{4,3,2,1,0:T(4,128)} copy(f32[8,5,64,4,64]{4,2,3,1,0:T(8,128)} %fusion.54) | data formatting | bytes 5242880 | tf_op jit(solution)/shard_map/lpkja,lkjatc->lkptc/dot_general | solution.py:83
  840.4 5.4 reshape.359
  845.8 3.3 convolution_convert_fusion
  851.2 33.4 %all_to_all.16 = bf16[8,5,16384]{2,1,0:T(8,128)(2,1)} all-to-all(bf16[8,5,16384]{2,1,0:T(8,128)(2,1)S(1)} %reshape.360), channel_id=1, replica_groups=mesh['seg'=4,'sec'=8] {'sec'}, dimensions={0} | all-to-all | bytes 2621440 | tf_op jit(solution)/shard_map/all_to_all | solution.py:92
  886.8 3.0 multiply_reduce_fusion.1
  891.0 20.1 %all-reduce.1 = (f32[]{:T(128)}, f32[]{:T(128)}) all-reduce(f32[]{:T(128)S(6)} %add.126, f32[]{:T(128)} %get-tuple-element.21), channel_id=1, replica_groups=mesh['seg'=4,'sec'=8] {'sec'}, use_global_device_ids=true, to_apply=%region_26.28 | all-reduce | flops 2 | bytes 16 | tf_op jit(solution)/shard_map/psum | solution.py:186
  915.5 17.7 %psum.111 = f32[]{:T(128)} all-reduce(f32[]{:T(128)} %get-tuple-element.63), channel_id=1, replica_groups=mesh['seg'=4,'sec'=8] {'sec'}, use_global_device_ids=true, to_apply=%region_32.34 | all-reduce | flops 1 | bytes 8 | tf_op jit(solution)/shard_map/psum | solution.py:171
  (163 shorter events, 55.3 us)
Async XLA Ops:
  7.2 66.1 %copy-start = (s32[64,4]{0,1:T(4,128)S(1)}, s32[64,4]{0,1:T(4,128)}, u32[]{:S(2)}) copy-start(s32[64,4]{0,1:T(4,128)} %param.21) | copy-start | bytes 3076
  7.2 125.1 %all-gather.3.cloned.1.call-start = ((), (), s32[]{:S(2)}) async-start(), calls=%async_computation.3 | async-start | bytes 2359296 | tf_op jit(solution)/shard_map/all_gather | solution.py:49
  7.9 117.2 %collective-permute-start.1 = (bf16[8,64,1920]{2,1,0:T(8,128)(2,1)}, bf16[8,64,1920]{2,1,0:T(8,128)(2,1)}, u32[]{:S(2)}, u32[]{:S(2)}) collective-permute-start(bf16[8,64,1920]{2,1,0:T(8,128)(2,1)} %bitcast.341), channel_id=1, source_target_pairs={{8,0},{16,8},{24,16},{9,1},{17,9},{25,17},{10,2},{18,10},{26,18},{... | collective-permute-start | bytes 5898248 | tf_op jit(solution)/shard_map/ppermute | solution.py:21
  31.5 11.8 %copy-start.17 = (bf16[30,4,30,4]{2,3,1,0:T(4,128)(2,1)S(1)}, bf16[30,4,30,4]{2,3,1,0:T(4,128)(2,1)}, u32[]{:S(2)}) copy-start(bf16[30,4,30,4]{2,3,1,0:T(4,128)(2,1)} %param.17) | copy-start | bytes 86404
  62.4 11.3 %copy-start.30 = (s32[64]{0:T(128)S(1)}, s32[64]{0:T(128)}, u32[]{:S(2)}) copy-start(s32[64]{0:T(128)} %param.20) | copy-start | bytes 772
  77.0 39.1 %copy-start.19 = (pred[8,256]{1,0:T(8,128)(4,1)}, pred[8,256]{1,0:T(8,128)(4,1)S(1)}, u32[]{:S(2)}) copy-start(pred[8,256]{1,0:T(8,128)(4,1)S(1)} %broadcast_compare_fusion) | copy-start | bytes 6148
  116.1 9.0 copy-start.16
  139.3 20.2 %copy-start.27 = (pred[8]{0:T(512)(128)(4,1)S(1)}, pred[8]{0:T(512)(128)(4,1)}, u32[]{:S(2)}) copy-start(pred[8]{0:T(512)(128)(4,1)} %get-tuple-element.56) | copy-start | bytes 28
  159.5 17.2 %copy-start.26 = (pred[8]{0:T(512)(128)(4,1)S(1)}, pred[8]{0:T(512)(128)(4,1)}, u32[]{:S(2)}) copy-start(pred[8]{0:T(512)(128)(4,1)} %get-tuple-element.74) | copy-start | bytes 28
  176.7 18.2 %copy-start.29 = (pred[8]{0:T(512)(128)(4,1)S(1)}, pred[8]{0:T(512)(128)(4,1)}, u32[]{:S(2)}) copy-start(pred[8]{0:T(512)(128)(4,1)} %get-tuple-element.52) | copy-start | bytes 28
  195.0 18.5 %copy-start.28 = (pred[8]{0:T(512)(128)(4,1)S(1)}, pred[8]{0:T(512)(128)(4,1)}, u32[]{:S(2)}) copy-start(pred[8]{0:T(512)(128)(4,1)} %get-tuple-element.76) | copy-start | bytes 28
  213.5 18.6 %copy-start.25 = (pred[8]{0:T(512)(128)(4,1)S(1)}, pred[8]{0:T(512)(128)(4,1)}, u32[]{:S(2)}) copy-start(pred[8]{0:T(512)(128)(4,1)} %get-tuple-element.48) | copy-start | bytes 28
  256.0 12.9 %copy-start.8 = (f32[8,64,4,64]{3,2,1,0:T(4,128)S(1)}, f32[8,64,4,64]{3,2,1,0:T(4,128)}, u32[]{:S(2)}) copy-start(f32[8,64,4,64]{3,2,1,0:T(4,128)} %squeeze.52) | copy-start | bytes 1572868
  256.0 12.9 %copy-start.23 = (pred[8,4,64]{2,1,0:T(4,128)(4,1)S(1)}, pred[8,4,64]{2,1,0:T(4,128)(4,1)}, u32[]{:S(2)}) copy-start(pred[8,4,64]{2,1,0:T(4,128)(4,1)} %iota_compare_fusion.4) | copy-start | bytes 6148
  256.0 12.9 %copy-start.24 = (pred[8,64]{1,0:T(8,128)(4,1)S(1)}, pred[8,64]{1,0:T(8,128)(4,1)}, u32[]{:S(2)}) copy-start(pred[8,64]{1,0:T(8,128)(4,1)} %copy.210) | copy-start | bytes 1540
  266.3 78.2 %collective-permute-start = (bf16[8,64,1920]{2,1,0:T(8,128)(2,1)S(1)}, bf16[8,64,1920]{2,1,0:T(8,128)(2,1)}, u32[]{:S(2)}, u32[]{:S(2)}) collective-permute-start(bf16[8,64,1920]{2,1,0:T(8,128)(2,1)S(1)} %reshape.345), channel_id=1, source_target_pairs={{0,8},{8,16},{16,24},{1,9},{9,17},{17,25},{2,10},{10,18},{18,26},{... | collective-permute-start | bytes 5898248 | tf_op jit(solution)/shard_map/ppermute | solution.py:21
  326.1 18.4 %copy-start.7 = (bf16[1,8,64,1920]{3,2,1,0:T(8,128)(2,1)S(1)}, bf16[1,8,64,1920]{3,2,1,0:T(8,128)(2,1)}, u32[]{:S(2)}) copy-start(bf16[1,8,64,1920]{3,2,1,0:T(8,128)(2,1)} %param.12) | copy-start | bytes 5898244
  376.6 10.4 %copy-start.18 = (s32[5,64]{1,0:T(8,128)S(1)}, s32[5,64]{1,0:T(8,128)}, u32[]{:S(2)}) copy-start(s32[5,64]{1,0:T(8,128)} %param.19) | copy-start | bytes 3844
  376.6 10.4 %copy-start.21 = (s32[8,2]{0,1:T(2,128)S(1)}, s32[8,2]{0,1:T(2,128)}, u32[]{:S(2)}) copy-start(s32[8,2]{0,1:T(2,128)} %concatenate.3) | copy-start | bytes 196
  376.6 10.4 %copy-start.22 = (s32[8,5,8]{2,1,0:T(8,128)S(1)}, s32[8,5,8]{2,1,0:T(8,128)}, u32[]{:S(2)}) copy-start(s32[8,5,8]{2,1,0:T(8,128)} %custom-call.10) | copy-start | bytes 3844
  379.9 56.5 %copy-start.2 = (f32[1,8,64,256]{3,2,1,0:T(8,128)S(1)}, f32[1,8,64,256]{3,2,1,0:T(8,128)}, u32[]{:S(2)}) copy-start(f32[1,8,64,256]{3,2,1,0:T(8,128)} %param.15) | copy-start | bytes 1572868
  380.0 56.5 %copy-start.20 = (pred[8,256]{1,0:T(8,128)(4,1)S(1)}, pred[8,256]{1,0:T(8,128)(4,1)}, u32[]{:S(2)}) copy-start(pred[8,256]{1,0:T(8,128)(4,1)} %copy-done.19) | copy-start | bytes 6148
  383.3 78.2 %copy-start.3 = (f32[1,8,64,256]{3,2,1,0:T(8,128)S(1)}, f32[1,8,64,256]{3,2,1,0:T(8,128)}, u32[]{:S(2)}) copy-start(f32[1,8,64,256]{3,2,1,0:T(8,128)} %param.16) | copy-start | bytes 1572868
  383.3 51.5 %all-to-all-start = ((bf16[8,5,16384]{2,1,0:T(8,128)(2,1)}), bf16[8,5,16384]{2,1,0:T(8,128)(2,1)S(1)}, u32[]{:S(2)}, u32[]{:S(2)}) async-start(bf16[8,5,16384]{2,1,0:T(8,128)(2,1)} %reshape.350), calls=%async_computation | async-start | bytes 4194304 | tf_op jit(solution)/shard_map/all_to_all | solution.py:92
  438.9 74.4 %copy-start.9 = (f32[8,64,256]{2,0,1:T(8,128)}, f32[8,64,256]{2,0,1:T(8,128)S(1)}, u32[]{:S(2)}) copy-start(f32[8,64,256]{2,0,1:T(8,128)S(1)} %get-tuple-element.71) | copy-start | bytes 1572868
  482.5 30.9 %copy-start.14 = (f32[8,64,256]{2,0,1:T(8,128)}, f32[8,64,256]{2,0,1:T(8,128)S(1)}, u32[]{:S(2)}) copy-start(f32[8,64,256]{2,0,1:T(8,128)S(1)} %get-tuple-element.45) | copy-start | bytes 1572868
  609.0 45.9 %copy-start.10 = (f32[8,64,256]{2,0,1:T(8,128)S(1)}, f32[8,64,256]{2,0,1:T(8,128)}, u32[]{:S(2)}) copy-start(f32[8,64,256]{2,0,1:T(8,128)} %copy-done.9) | copy-start | bytes 1572868
  651.6 30.0 %copy-start.11 = (f32[8,64,256]{2,0,1:T(8,128)S(1)}, f32[8,64,256]{2,0,1:T(8,128)}, u32[]{:S(2)}) copy-start(f32[8,64,256]{2,0,1:T(8,128)} %copy-done.9) | copy-start | bytes 1572868
  651.6 30.0 %copy-start.15 = (f32[8,64,256]{2,0,1:T(8,128)S(1)}, f32[8,64,256]{2,0,1:T(8,128)}, u32[]{:S(2)}) copy-start(f32[8,64,256]{2,0,1:T(8,128)} %copy-done.14) | copy-start | bytes 1572868
  654.9 47.2 %copy-start.4 = (f32[1,8,64,256]{3,2,1,0:T(8,128)S(1)}, f32[1,8,64,256]{3,2,1,0:T(8,128)}, u32[]{:S(2)}) copy-start(f32[1,8,64,256]{3,2,1,0:T(8,128)} %param.16) | copy-start | bytes 1572868
  683.8 69.7 %copy-start.5 = (f32[8,64,256]{2,0,1:T(8,128)}, f32[8,64,256]{2,0,1:T(8,128)S(1)}, u32[]{:S(2)}) copy-start(f32[8,64,256]{2,0,1:T(8,128)S(1)} %get-tuple-element.43) | copy-start | bytes 1572868
  724.5 29.0 %copy-start.12 = (f32[8,64,256]{2,0,1:T(8,128)}, f32[8,64,256]{2,0,1:T(8,128)S(1)}, u32[]{:S(2)}) copy-start(f32[8,64,256]{2,0,1:T(8,128)S(1)} %get-tuple-element.40) | copy-start | bytes 1572868
  849.2 37.6 %copy-start.6 = (f32[8,64,256]{2,0,1:T(8,128)S(1)}, f32[8,64,256]{2,0,1:T(8,128)}, u32[]{:S(2)}) copy-start(f32[8,64,256]{2,0,1:T(8,128)} %copy-done.5) | copy-start | bytes 1572868
  851.1 82.7 %copy-start.1 = (s32[64,4]{0,1:T(4,128)S(1)}, s32[64,4]{0,1:T(4,128)}, u32[]{:S(2)}) copy-start(s32[64,4]{0,1:T(4,128)} %param.21) | copy-start | bytes 3076
  884.5 28.2 %copy-start.13 = (f32[8,64,256]{2,0,1:T(8,128)S(1)}, f32[8,64,256]{2,0,1:T(8,128)}, u32[]{:S(2)}) copy-start(f32[8,64,256]{2,0,1:T(8,128)} %copy-done.12) | copy-start | bytes 1572868
Sparse Core Ops, SparseCore 0:
  10.1 51.9 all-gather.2
where the time goes:
time: 953 us; the launch traced here: 942 us
  matrix products  381 us (40%)
  blocking collectives  271 us (28%)
  local copies, waits for them, and re-layouts  199 us (21%)
  waiting for transfers between devices  36.9 us (4%)
  between operations  27.1 us (3%)
  other arithmetic  20.5 us (2%)
    dot_general x3, matrix products, apply_operator(): jnp.einsum('wtvs,lasvc->lwatc', channel_mix, right_product, preferred_ele...  141 us
    dot_general x5, matrix products, build_environment(): jnp.einsum('lpte,lptvb->levb', shifted_site, carried, preferred_element_t...  96.4 us
    all_to_all x2, blocking collectives, apply_operator(): lax.all_to_all(outgoing, 'sec', split_axis=0, concat_axis=0, tiled=True)  74 us
    psum x3, blocking collectives, rayleigh(): return lax.psum(jnp.sum(vector * result), 'sec') / total_entries  57.3 us
    convert_element_type x3, local copies, waits for them, and re-layouts, apply_operator(): mixed_product = jnp.einsum('wtvs,lasvc->lwatc', channel_mix, right_produc...  54.7 us
    dot_general x5, matrix products, build_environment(): jnp.einsum('jtvs,lpjsb->lptvb', channel_split[charge], contracted[:, :, c...  46.6 us
    psum x2, blocking collectives, on_device(): lax.psum((jnp.sum(current * product), jnp.sum(direction * applied), jnp.s...  40.3 us
    psum x2, blocking collectives, on_device(): lax.psum(jnp.sum(correction * correction), 'sec') / total_entries  37.7 us
  transfers between devices with their start and end apart: 4, of which 1 were waited for; matrix products, arithmetic and copies ran while one was open for 20% of the time, Pallas kernels for 0%

commit v1 on v0

v1 whole, which is shorter than its diff:
```python
import functools

import jax
import jax.numpy as jnp
from jax import lax
from jax.experimental import pallas as pl
from jax.experimental.pallas import tpu as pltpu
from jax.sharding import PartitionSpec as P

W = 30
D = 4
B = 64
SEC_DEV = 8
CLASSES = 5
ITERS = 2


EPSILON = 1e-06
HIGHEST_PRECISION = lax.Precision.HIGHEST


def passed_along(block, axis, distance):
    devices = range(lax.axis_size(axis))
    route = [(i - distance, i) for i in devices if i - distance in devices]
    return lax.ppermute(block, axis, route)


def live_masks(left_sizes, right_sizes, offset):
    row_limit = lax.dynamic_slice_in_dim(left_sizes, offset, SEC_DEV, 0)
    column_limit = lax.dynamic_slice_in_dim(right_sizes, offset, SEC_DEV, 0)
    row_live = jnp.arange(B, dtype=jnp.int32)[None, :] < row_limit[:, None]
    column_live = jnp.arange(B, dtype=jnp.int32)[None, None, :] < column_limit[:, :, None]
    joined_live = row_live[:, :, None, None] & column_live[:, None, :, :]
    return joined_live.astype(jnp.float32).reshape(SEC_DEV, B, D * B)


def send_order(group_total):
    return sorted(range(1, group_total), key=lambda step: -min(step, group_total - step))


def pair_tables(sector_shift, group, group_total):
    target_list = lax.dynamic_slice_in_dim(sector_shift, group * SEC_DEV, SEC_DEV, 1).T.reshape(
        SEC_DEV * CLASSES
    )
    steps = send_order(group_total)
    place_of = [group_total - 1] * group_total
    for place, step in enumerate(steps):
        place_of[step] = place
    place_of = jnp.array(place_of, dtype=jnp.int32)
    step_list = (target_list // SEC_DEV - group + group_total) % group_total
    one_hot = step_list[:, None] == jnp.arange(group_total, dtype=jnp.int32)[None, :]
    place_list = jnp.sum(jnp.where(one_hot, place_of[None, :], 0), axis=1)
    order = jnp.arange(SEC_DEV * CLASSES, dtype=jnp.int32)
    sort_key = place_list * (SEC_DEV * CLASSES) + order
    position = jnp.sum((sort_key[None, :] < sort_key[:, None]).astype(jnp.int32), axis=1)
    place_start = jnp.sum(
        (place_list[:, None] < jnp.arange(group_total, dtype=jnp.int32)[None, :]).astype(jnp.int32), axis=0
    )
    own_start = jnp.sum((place_list[None, :] < place_list[:, None]).astype(jnp.int32), axis=1)
    return target_list, place_list, position, place_start, position - own_start


def routing_tables(sector_shift, my_group, group_total, capacity):
    pairs = SEC_DEV * CLASSES
    groups = jnp.arange(group_total, dtype=jnp.int32)
    targets, places, positions, starts, ranks = jax.vmap(
        lambda group: pair_tables(sector_shift, group, group_total)
    )(groups)
    mine = groups == my_group
    my_position = jnp.sum(jnp.where(mine[:, None], positions, 0), axis=0)
    my_start = jnp.sum(jnp.where(mine[:, None], starts, 0), axis=0)
    index = jnp.arange(pairs, dtype=jnp.int32)
    sorted_pair = jnp.sum(jnp.where(my_position[None, :] == index[:, None], index[None, :], 0), axis=1)
    slot_source = (
        my_start[: group_total - 1, None] + jnp.arange(capacity, dtype=jnp.int32)[None, :]
    ).reshape(-1)
    slot_source = jnp.minimum(slot_source, pairs - 1)
    local = targets - my_group * SEC_DEV
    slots = (group_total - 1) * capacity
    value = jnp.where(mine[:, None], slots + positions, places * capacity + ranks)
    wanted = jnp.arange(SEC_DEV, dtype=jnp.int32)
    class_of = index % CLASSES
    hit = (local[None, None, :, :] == wanted[:, None, None, None]) & (
        class_of[None, None, None, :] == jnp.arange(CLASSES, dtype=jnp.int32)[None, :, None, None]
    )
    source = jnp.sum(jnp.where(hit, value[None, None], 0), axis=(2, 3)).reshape(pairs)
    from_self = (source >= slots).astype(jnp.int32)
    arrived_slot = jnp.where(from_self == 1, 0, source)
    own_position = jnp.where(from_self == 1, source - slots, 0)
    return sorted_pair, slot_source, from_self, arrived_slot, own_position


def gate_kernel(mix_ref, right_ref, gate_ref, spread):
    sites, channel_sites, _ = mix_ref.shape
    classes = gate_ref.shape[0]
    halves = right_ref.shape[2] // 128
    bond = 2 * halves
    per_class = channel_sites // classes
    low_lanes = lax.broadcasted_iota(jnp.int32, (halves, 128), 1) < 64
    for site in range(sites):
        mixed = jnp.dot(mix_ref[site], right_ref[0], preferred_element_type=jnp.float32)
        for half in range(halves):
            spread[half * channel_sites : (half + 1) * channel_sites, :] = mixed[
                :, half * 128 : (half + 1) * 128
            ]

        def one_class(charge, carry):
            for pair in range(per_class // 2):
                first = charge * per_class + 2 * pair
                one = spread[pl.ds(first, halves, stride=channel_sites), :]
                two = spread[pl.ds(first + 1, halves, stride=channel_sites), :]
                upper = jnp.where(low_lanes, one, pltpu.roll(two, 64, 1))
                lower = jnp.where(low_lanes, pltpu.roll(one, 64, 1), two)
                lanes = slice(pair * 128, (pair + 1) * 128)
                gate_ref[charge, site * bond : site * bond + halves, lanes] = upper.astype(jnp.bfloat16)
                gate_ref[charge, site * bond + halves : (site + 1) * bond, lanes] = lower.astype(
                    jnp.bfloat16
                )
            return carry

        lax.fori_loop(0, classes, one_class, 0)


def environment_kernel(shift_ref, mix_ref, left_ref, site_ref, every_ref, out_ref, spread, turned):
    classes, bond, per_columns = out_ref.shape
    per_class = per_columns // bond
    mixed_rows = mix_ref.shape[0]
    sites = every_ref.shape[2] // bond
    channels = classes * per_class
    halves = bond // 2
    sector = pl.program_id(0)
    sectors = pl.num_programs(0)
    low_lanes = lax.broadcasted_iota(jnp.int32, (halves, 128), 1) < 64
    for charge in range(classes):
        shifted = every_ref[shift_ref[charge * sectors + sector]]
        joined = lax.dot_general(
            shifted,
            left_ref[0, :, charge * per_columns : (charge + 1) * per_columns],
            (((0,), (0,)), ((), ())),
            preferred_element_type=jnp.float32,
        )
        for site in range(sites):
            for pair in range(per_class // 2):
                lanes = slice(pair * 128, (pair + 1) * 128)
                one = joined[site * bond : site * bond + halves, lanes]
                two = joined[site * bond + halves : (site + 1) * bond, lanes]
                row = (charge * per_class + 2 * pair) * sites + site
                spread[pl.ds(row, halves, stride=mixed_rows), :] = jnp.where(
                    low_lanes, one, pltpu.roll(two, 64, 1)
                )
                spread[pl.ds(row + sites, halves, stride=mixed_rows), :] = jnp.where(
                    low_lanes, pltpu.roll(one, 64, 1), two
                )

    def mix_two(half, carry):
        base = pl.multiple_of(half * 2 * mixed_rows, 8)
        after = pl.multiple_of(base + mixed_rows, 8)
        both = jnp.concatenate(
            [spread[pl.ds(base, mixed_rows), :], spread[pl.ds(after, mixed_rows), :]], axis=1
        ).astype(jnp.bfloat16)
        mixed = jnp.dot(mix_ref[...], both, preferred_element_type=jnp.float32)
        spread[pl.ds(base, mixed_rows), :] = mixed[:, :128]
        spread[pl.ds(after, mixed_rows), :] = mixed[:, 128:]
        return carry

    lax.fori_loop(0, halves // 2, mix_two, 0, unroll=4)
    for channel in range(channels):
        for pair in range(sites // 2):
            row = channel * sites + 2 * pair
            one = spread[pl.ds(row, halves, stride=mixed_rows), :]
            two = spread[pl.ds(row + 1, halves, stride=mixed_rows), :]
            lanes = slice(pair * 128, (pair + 1) * 128)
            turned[channel * bond : channel * bond + halves, lanes] = jnp.where(
                low_lanes, one, pltpu.roll(two, 64, 1)
            ).astype(jnp.bfloat16)
            turned[channel * bond + halves : (channel + 1) * bond, lanes] = jnp.where(
                low_lanes, pltpu.roll(one, 64, 1), two
            ).astype(jnp.bfloat16)
    for charge in range(classes):
        rows = slice(charge * per_columns, (charge + 1) * per_columns)
        built = jnp.dot(turned[rows, :], site_ref[0], preferred_element_type=jnp.float32)
        for pair in range(per_class // 2):
            one = built[2 * pair * bond : (2 * pair + 1) * bond]
            two = built[(2 * pair + 1) * bond : (2 * pair + 2) * bond]
            out_ref[charge, :, pair * 128 : (pair + 1) * 128] = jnp.concatenate(
                [one, two], axis=1
            ).astype(jnp.bfloat16)


def build_environment(environment, site_blocks, channel_mix, sector_shift, offset):
    every_site = lax.all_gather(site_blocks, "sec", axis=0, tiled=True)
    sectors = environment.shape[0]
    targets = lax.dynamic_slice_in_dim(sector_shift, offset, sectors, 1).reshape(-1)
    mix = channel_mix.transpose(2, 3, 0, 1).reshape(W * D, W * D)
    own = site_blocks.reshape(sectors, B, D, B).transpose(0, 2, 1, 3).reshape(sectors, D * B, B)
    per_columns = W // CLASSES * B
    return pl.pallas_call(
        environment_kernel,
        grid=(sectors,),
        in_specs=[
            pl.BlockSpec(memory_space=pltpu.SMEM),
            pl.BlockSpec((W * D, W * D), lambda sector: (0, 0)),
            pl.BlockSpec((1, B, W * B), lambda sector: (sector, 0, 0)),
            pl.BlockSpec((1, D * B, B), lambda sector: (sector, 0, 0)),
            pl.BlockSpec(every_site.shape, lambda sector: (0, 0, 0)),
        ],
        out_specs=pl.BlockSpec((CLASSES, B, per_columns), lambda sector: (sector, 0, 0)),
        out_shape=jax.ShapeDtypeStruct((sectors * CLASSES, B, per_columns), jnp.bfloat16),
        scratch_shapes=[
            pltpu.VMEM((B // 2 * W * D, 2 * B), jnp.float32),
            pltpu.VMEM((W * B, D * B), jnp.bfloat16),
        ],
        compiler_params=pltpu.CompilerParams(vmem_limit_bytes=32 * 1024 * 1024),
        cost_estimate=pl.CostEstimate(
            flops=8 * sectors * W * D * W * D * B * B, bytes_accessed=6000000, transcendentals=0
        ),
    )(targets, mix, environment, own, every_site)


def build_gate(right_used, channel_mix):
    sectors = right_used.shape[0]
    halves = B // 2
    right_split = right_used.reshape(sectors, 2, halves, W, B).transpose(0, 3, 2, 1, 4)
    right_split = right_split.reshape(sectors, W, B * B)
    mix = channel_mix.transpose(3, 0, 1, 2).reshape(D, W * D, W)
    shape = (sectors * CLASSES, D * B, W // CLASSES * D * B)
    return pl.pallas_call(
        gate_kernel,
        grid=(sectors,),
        in_specs=[
            pl.BlockSpec((D, W * D, W), lambda sector: (0, 0, 0)),
            pl.BlockSpec((1, W, B * B), lambda sector: (sector, 0, 0)),
        ],
        out_specs=pl.BlockSpec((CLASSES,) + shape[1:], lambda sector: (sector, 0, 0)),
        out_shape=jax.ShapeDtypeStruct(shape, jnp.bfloat16),
        scratch_shapes=[pltpu.VMEM((halves * W * D, 2 * B), jnp.float32)],
        compiler_params=pltpu.CompilerParams(vmem_limit_bytes=32 * 1024 * 1024),
        cost_estimate=pl.CostEstimate(
            flops=2 * sectors * D * W * D * W * B * B, bytes_accessed=36000000, transcendentals=0
        ),
    )(mix, right_split)


def davidson_kernel(
    n,
    capacity,
    total_entries,
    pair_ref,
    slot_ref,
    self_ref,
    arrived_ref,
    own_ref,
    mask_ref,
    start_ref,
    precondition_ref,
    left_ref,
    gate_ref,
    state_ref,
    energy_ref,
    current,
    applied,
    direction,
    product,
    low,
    stacked,
    partial,
    outgoing,
    incoming,
    row_send,
    row_all,
    send_sem,
    recv_sem,
    row_send_sem,
    row_recv_sem,
):
    pairs = left_ref.shape[0]
    sectors, rows, columns = current.shape
    classes = pairs // sectors
    channels = left_ref.shape[2] // rows
    steps = send_order(n)
    me = lax.axis_index("sec")

    barrier = pltpu.get_barrier_semaphore()
    for step in steps:
        pl.semaphore_signal(
            barrier,
            inc=1,
            device_id={"sec": lax.rem(me + step, n)},
            device_id_type=pl.DeviceIdType.MESH,
        )
    pl.semaphore_wait(barrier, n - 1)

    def fold(values):
        eight = jnp.sum(values.reshape(rows // 8, 8, columns), axis=0)
        return eight[:, : columns // 2] + eight[:, columns // 2 :]

    def all_sums(turn, count, products):
        zero = jnp.zeros((8, columns // 2), jnp.float32)

        def body(sector, sums):
            return tuple(total + fold(term) for total, term in zip(sums, products(sector)))

        sums = lax.fori_loop(0, sectors, body, (zero,) * count)
        for entry in range(8):
            if entry < count:
                row_send[turn, entry : entry + 1, :] = jnp.sum(sums[entry], axis=0, keepdims=True)
            else:
                row_send[turn, entry : entry + 1, :] = zero[0:1]
        copies = []
        for place, step in enumerate(steps):
            copies.append(
                pltpu.make_async_remote_copy(
                    src_ref=row_send.at[turn],
                    dst_ref=row_all.at[turn, me],
                    send_sem=row_send_sem.at[turn, place],
                    recv_sem=row_recv_sem.at[turn, place],
                    device_id={"sec": lax.rem(me + step, n)},
                    device_id_type=pl.DeviceIdType.MESH,
                )
            )
            copies[-1].start()
        row_all[turn, me] = row_send[turn]
        for copy in copies:
            copy.wait()
        whole = row_all[turn, 0]
        for group in range(1, n):
            whole = whole + row_all[turn, group]
        whole = jnp.sum(whole, axis=1, keepdims=True) / total_entries
        return [whole[entry : entry + 1, :] for entry in range(count)]

    def operator(turn, result):
        def one_pair(position, carry):
            pair = pair_ref[position]
            sector = pair_ref[pairs + position]
            mixed = jnp.dot(low[sector], gate_ref[pair], preferred_element_type=jnp.float32)
            for channel in range(channels):
                stacked[channel * rows : (channel + 1) * rows, :] = mixed[
                    :, channel * columns : (channel + 1) * columns
                ].astype(jnp.bfloat16)
            partial[position] = jnp.dot(
                left_ref[pair], stacked[...], preferred_element_type=jnp.float32
            )
            return carry

        copies = []
        done = 0
        for place, step in enumerate(steps):
            upto = min((place + 1) * capacity, pairs)
            lax.fori_loop(done, upto, one_pair, 0)
            done = upto
            for rank in range(capacity):
                outgoing[turn, place, rank] = partial[slot_ref[place * capacity + rank]].astype(
                    jnp.bfloat16
                )
            copies.append(
                pltpu.make_async_remote_copy(
                    src_ref=outgoing.at[turn, place],
                    dst_ref=incoming.at[turn, place],
                    send_sem=send_sem.at[turn, place],
                    recv_sem=recv_sem.at[turn, place],
                    device_id={"sec": lax.rem(me + step, n)},
                    device_id_type=pl.DeviceIdType.MESH,
                )
            )
            copies[-1].start()
        if done < pairs:
            lax.fori_loop(done, pairs, one_pair, 0)
        for copy in copies:
            copy.wait()
        landed = incoming.at[turn]

        def gather(sector, carry):
            total = jnp.zeros((rows, columns), jnp.float32)
            for charge in range(classes):
                entry = sector * classes + charge
                slot = arrived_ref[entry]
                came = landed[arrived_ref[pairs + entry], slot].astype(jnp.float32)
                own = partial[own_ref[entry]]
                own_part = jnp.broadcast_to(self_ref[entry], (rows, columns)) == 1
                total = total + jnp.where(own_part, own, came)
            result[sector] = mask_ref[sector] * total
            return carry

        lax.fori_loop(0, sectors, gather, 0)

    def first(sector, carry):
        current[sector] = mask_ref[sector] * start_ref[sector]
        return carry

    lax.fori_loop(0, sectors, first, 0)
    (start_square,) = all_sums(0, 1, lambda s: (current[s] * current[s],))
    start_scale = 1.0 / jnp.sqrt(start_square + EPSILON)

    def normalise(sector, carry):
        value = current[sector] * start_scale
        current[sector] = value
        low[sector] = value.astype(jnp.bfloat16)
        return carry

    lax.fori_loop(0, sectors, normalise, 0)
    operator(0, applied)
    energy = None
    for iteration in range(ITERS):

        def shaped(sector):
            one, two = current[sector], applied[sector]
            weight = precondition_ref[sector]
            weighted_one, weighted_two = weight * one, weight * two
            return (
                one * two,
                one * one,
                one * weighted_two,
                one * weighted_one,
                weighted_two * weighted_two,
                weighted_two * weighted_one,
                weighted_one * weighted_one,
            )

        sums = all_sums(1 + 2 * iteration, 7, shaped)
        rho = sums[0]
        correlation = sums[2] - rho * sums[3]
        square = sums[4] - 2.0 * rho * sums[5] + rho * rho * sums[6]
        square = square - 2.0 * correlation * correlation + correlation * correlation * sums[1]
        scale = 1.0 / jnp.sqrt(jnp.maximum(square, 0.0) + EPSILON)

        def correct(sector, carry):
            one = current[sector]
            value = precondition_ref[sector] * (applied[sector] - rho * one)
            value = (value - correlation * one) * scale
            direction[sector] = value
            low[sector] = value.astype(jnp.bfloat16)
            return carry

        lax.fori_loop(0, sectors, correct, 0)
        operator(1 + iteration, product)
        sums = all_sums(
            2 + 2 * iteration,
            3,
            lambda s: (current[s] * product[s], direction[s] * applied[s], direction[s] * product[s]),
        )
        cross = 0.5 * (sums[0] + sums[1])
        far = sums[2]
        across, along = -2.0 * cross, far - rho
        largest = jnp.maximum(jnp.abs(across), jnp.abs(along))
        still = largest == 0.0
        safe = jnp.where(still, 1.0, largest)
        across, along = across / safe, jnp.where(still, 1.0, along / safe)
        length = jnp.sqrt(across * across + along * along)
        bigger = jnp.sqrt(0.5 * (length + jnp.abs(along)) / length)
        smaller = 0.5 * jnp.abs(across) / (length * bigger)
        ahead = along >= 0.0
        cosine = jnp.where(ahead, bigger, smaller)
        sine = jnp.where(ahead, smaller, bigger)
        sine = jnp.where(across > 0.0, sine, -sine)
        energy = cosine * cosine * rho + 2.0 * cosine * sine * cross + sine * sine * far
        last = iteration == ITERS - 1

        def rotate(sector, carry):
            value = cosine * current[sector] + sine * direction[sector]
            if last:
                state_ref[sector] = value
            else:
                current[sector] = value
                applied[sector] = cosine * applied[sector] + sine * product[sector]
            return carry

        lax.fori_loop(0, sectors, rotate, 0)
    energy_ref[...] = jnp.broadcast_to(energy, energy_ref.shape)


def davidson(tables, live_mask, start, precondition, left_pairs, gate, group_total, capacity):
    pairs = left_pairs.shape[0]
    sectors, rows, columns = start.shape
    sorted_pair, slot_source, from_self, arrived_slot, own_position = tables
    sorted_pair = jnp.concatenate([sorted_pair, sorted_pair // CLASSES])
    arrived_slot = jnp.concatenate([arrived_slot % capacity, arrived_slot // capacity])
    turns = ITERS + 1
    rounds = 2 * ITERS + 1
    others = group_total - 1
    smem = pl.BlockSpec(memory_space=pltpu.SMEM)
    vmem = pl.BlockSpec(memory_space=pltpu.VMEM)
    vector = pltpu.VMEM((sectors, rows, columns), jnp.float32)
    kernel = functools.partial(
        davidson_kernel, group_total, capacity, float(group_total * sectors * rows * columns)
    )
    return pl.pallas_call(
        kernel,
        out_shape=(
            jax.ShapeDtypeStruct(start.shape, jnp.float32),
            jax.ShapeDtypeStruct((8, 128), jnp.float32),
        ),
        in_specs=[smem] * 5 + [vmem] * 5,
        out_specs=(vmem, vmem),
        scratch_shapes=[
            vector,
            vector,
            vector,
            vector,
            pltpu.VMEM((sectors, rows, columns), jnp.bfloat16),
            pltpu.VMEM((left_pairs.shape[2], columns), jnp.bfloat16),
            pltpu.VMEM((pairs, rows, columns), jnp.float32),
            pltpu.VMEM((turns, others, capacity, rows, columns), jnp.bfloat16),
            pltpu.VMEM((turns, others, capacity, rows, columns), jnp.bfloat16),
            pltpu.VMEM((rounds, 8, columns // 2), jnp.float32),
            pltpu.VMEM((rounds, group_total, 8, columns // 2), jnp.float32),
            pltpu.SemaphoreType.DMA((turns, others)),
            pltpu.SemaphoreType.DMA((turns, others)),
            pltpu.SemaphoreType.DMA((rounds, others)),
            pltpu.SemaphoreType.DMA((rounds, others)),
        ],
        compiler_params=pltpu.CompilerParams(
            collective_id=0, has_side_effects=True, vmem_limit_bytes=58 * 1024 * 1024
        ),
    )(
        sorted_pair,
        slot_source,
        from_self,
        arrived_slot,
        own_position,
        live_mask,
        start,
        precondition,
        left_pairs,
        gate,
    )


def on_device(
    left_environment,
    right_environment,
    site_previous,
    state_start,
    preconditioner,
    channel_tensor,
    channel_mask,
    sector_shift,
    left_sizes,
    right_sizes,
):
    group_total = lax.axis_size("sec")
    my_group = lax.axis_index("sec")
    offset = my_group * SEC_DEV
    capacity = (CLASSES * SEC_DEV + group_total - 1) // group_total
    channel_mix = channel_tensor * channel_mask.astype(jnp.bfloat16)[:, None, :, None]
    live_mask = live_masks(left_sizes, right_sizes, offset)
    own_left = left_environment[0]
    position = lax.axis_index("seg")
    came_right = passed_along(right_environment[0], "seg", -1)
    right_used = jnp.where(position == lax.axis_size("seg") - 1, right_environment[0], came_right)
    fresh = build_environment(own_left, site_previous[0], channel_mix, sector_shift, offset)
    handed = passed_along(fresh, "seg", 1)
    own_pairs = (
        own_left.reshape(SEC_DEV, B, CLASSES, W // CLASSES * B)
        .transpose(0, 2, 1, 3)
        .reshape(SEC_DEV * CLASSES, B, W // CLASSES * B)
    )
    left_pairs = jnp.where(position == 0, own_pairs, handed)
    gate = build_gate(right_used, channel_mix)
    tables = routing_tables(sector_shift, my_group, group_total, capacity)
    state, energy = davidson(
        tables, live_mask, state_start[0], preconditioner[0], left_pairs, gate, group_total, capacity
    )
    return (state[None], energy[0, 0:1])


def solution(mesh):
    in_specs = (
        P("seg", "sec", None, None),
        P("seg", "sec", None, None),
        P("seg", "sec", None, None),
        P("seg", "sec", None, None),
        P("seg", "sec", None, None),
        P(),
        P(),
        P(),
        P(),
        P(),
    )
    out_specs = (P("seg", "sec", None, None), P("seg"))
    return jax.shard_map(
        on_device, mesh=mesh, in_specs=in_specs, out_specs=out_specs, check_vma=False
    )
```

time: 953 us -> 293 us (0.31)
  matrix products: 381 us -> 0 us
  blocking collectives: 271 us -> 0 us
  Pallas kernels: 0 us -> 190 us
  local copies, waits for them, and re-layouts: 199 us -> 56.1 us
  waiting for transfers between devices: 36.9 us -> 16.3 us
  between operations: 27.1 us -> 14.2 us
    dot_general x27 -> x0, matrix products: 381 us -> none  [the longest x3 141 us: apply_operator(): jnp.einsum('wtvs,lasvc->lwatc', channel_mix, right_product, preferred_ele...]
    psum x10 -> x0, blocking collectives: 197 us -> none  [the longest x3 57.3 us: rayleigh(): return lax.psum(jnp.sum(vector * result), 'sec') / total_entries]
    pallas_call x0 -> x3, Pallas kernels: none -> 190 us  [the longest x1 132 us: davidson(): pl.pallas_call(kernel, out_shape=(jax.ShapeDtypeStruct(start.shape, jnp.f...]
    all_to_all x2 -> x0, blocking collectives: 74 us -> none  [apply_operator(): lax.all_to_all(outgoing, 'sec', split_axis=0, concat_axis=0, tiled=True)]
    convert_element_type x5 -> x0, local copies, waits for them, and re-layouts: 59.3 us -> none  [the longest x3 54.7 us: apply_operator(): mixed_product = jnp.einsum('wtvs,lasvc->lwatc', channel_mix, right_produc...]
    reshape x18 -> x7, local copies, waits for them, and re-layouts: 58.8 us -> 21.7 us  [the longest x2 13.3 us: build_gate(): right_split = right_split.reshape(sectors, W, B * B)]
    all_to_all x1 -> x0, waiting for transfers between devices: 36.2 us -> none  [apply_operator(): lax.all_to_all(outgoing, 'sec', split_axis=0, concat_axis=0, tiled=True)]
    dot_general x3 -> x0, local copies, waits for them, and re-layouts: 28.6 us -> none  [apply_operator(): jnp.einsum('lpkja,lkjatc->lkptc', left_split, grouped, preferred_element_...]
  transfers between devices with their start and end apart: 4 -> 3, of which waited for: 1 -> 1; matrix products, arithmetic and copies ran while one was open for 20% -> 21% of each run, Pallas kernels for 0% -> 20%
where the time goes in v1:
time: 293 us; the launch traced here: 292 us
  Pallas kernels  190 us (65%)
  local copies, waits for them, and re-layouts  56.1 us (19%)
  waiting for transfers between devices  16.3 us (6%)
  between operations  14.2 us (5%)
  other arithmetic  11.3 us (4%)
  starting transfers between devices  3.87 us (1%)
    pallas_call x1, Pallas kernels, davidson(): pl.pallas_call(kernel, out_shape=(jax.ShapeDtypeStruct(start.shape, jnp.f...  132 us
    pallas_call x1, Pallas kernels, build_gate(): pl.pallas_call(gate_kernel, grid=(sectors,), in_specs=[pl.BlockSpec((D, W...  36.5 us
    pallas_call x1, Pallas kernels, build_environment(): pl.pallas_call(environment_kernel, grid=(sectors,), in_specs=[pl.BlockSpe...  21.2 us
    gather x24, local copies, waits for them, and re-layouts  16 us
    all_gather x1, waiting for transfers between devices, build_environment(): every_site = lax.all_gather(site_blocks, 'sec', axis=0, tiled=True)  15.6 us
    reshape x2, local copies, waits for them, and re-layouts, build_gate(): right_split = right_split.reshape(sectors, W, B * B)  13.3 us
  transfers between devices with their start and end apart: 3, of which 1 were waited for; matrix products, arithmetic and copies ran while one was open for 21% of the time, Pallas kernels for 20%

profile of v1, /device:TPU:0, one launch (start us, length us, event | category | flops | bytes accessed | tf_op | source)
XLA Modules:
  0.0 291.6 jit_solution(14904370097903691845)
XLA Ops:
  7.2 0.7 all-gather.3.cloned.1.call-update
  7.9 1.3 collective-permute-start.1
  9.2 1.2 reshape_squeeze.7
  10.5 0.7 dynamic_slice.9
  11.3 0.1 copy.37
  11.4 0.1 lt.125
  11.5 0.8 constant_dynamic-slice_fusion.2
  12.2 0.1 reshape.228.shift_ref
  12.3 0.7 convert_element_type.24
  13.1 0.1 lt.128
  13.2 16.0 %while.1 = (s32[]{:T(128)}, s32[5,64]{1,0:T(8,128)}, s32[8,2]{0,1:T(2,128)S(1)}, s32[8,5,8]{2,1,0:T(8,128)S(1)}, s32[]{:T(128)}) while((s32[]{:T(128)}, s32[5,64]{1,0:T(8,128)}, s32[8,2]{0,1:T(2,128)S(1)}, s32[8,5,8]{2,1,0:T(8,128)S(1)}, s32[]{:T(128)}) %tuple.26), condition=%wide.while_cond, body=%wide.while_body.sunk | while | flops 2 | bytes 4361 | solution.py:42
  13.3 0.5 slice.20
  13.8 1.4 bitcast_dynamic-update-slice_fusion.2
  15.3 0.5 slice.20
  15.8 1.4 bitcast_dynamic-update-slice_fusion.2
  17.3 0.5 slice.20
  17.8 1.4 bitcast_dynamic-update-slice_fusion.2
  19.3 0.5 slice.20
  19.8 1.4 bitcast_dynamic-update-slice_fusion.2
  21.3 0.5 slice.20
  21.8 1.4 bitcast_dynamic-update-slice_fusion.2
  23.3 0.5 slice.20
  23.8 1.4 bitcast_dynamic-update-slice_fusion.2
  25.3 0.5 slice.20
  25.8 1.4 bitcast_dynamic-update-slice_fusion.2
  27.3 0.5 slice.20
  27.8 1.4 bitcast_dynamic-update-slice_fusion.2
  29.2 0.1 copy.36
  29.3 0.1 reshape.225
  29.4 0.9 select_reduce_fusion.1
  30.3 0.2 convert_reduce_fusion.2
  30.5 0.1 select_reduce_fusion.3
  30.6 0.1 add_minimum_fusion
  30.7 0.7 min.10.slot_ref
  31.3 0.3 convert_reduce_fusion
  31.7 0.3 convert_reduce_fusion.1
  32.0 0.1 add_select_fusion.2
  32.1 0.8 select_reduce_fusion
  32.9 0.1 reshape.226
  33.0 1.0 multiply_bitcast_fusion
  34.0 0.1 copy.40
  34.1 2.7 copy.39
  36.8 2.7 reshape.229.mix_ref
  39.6 3.4 %reshape_squeeze.6 = bf16[8,64,5,384]{3,2,1,0:T(8,128)(2,1)} reshape(bf16[1,8,64,1920]{3,2,1,0:T(8,128)(2,1)S(1)} %copy-done.2) | data formatting | bytes 3932160 | tf_op jit(solution)/shard_map/reshape;squeeze | solution.py:553
  43.0 3.6 %copy.38 = bf16[8,5,64,384]{3,2,1,0:T(8,128)(2,1)} copy(bf16[8,5,64,384]{3,1,2,0:T(8,128)(2,1)} %bitcast.39) | data formatting | bytes 3932160 | tf_op jit(solution)/shard_map/transpose | solution.py:554
  46.6 0.1 select_reduce_fusion.2
  46.7 15.6 %all-gather.3.cloned.1.call-done = bf16[1,64,64,256]{3,2,0,1:T(8,128)(2,1)} async-done(((bf16[1,8,64,256]{3,2,0,1:T(8,128)(2,1)}), bf16[1,64,64,256]{3,2,0,1:T(8,128)(2,1)}) %all-gather.3.cloned.1.call-update) | async-done | bytes 2097168 | tf_op jit(solution)/shard_map/all_gather | solution.py:191
  62.2 1.6 copy-done.3
  63.8 21.2 %shard_map.122 = bf16[40,64,384]{2,1,0:T(8,128)(2,1)} custom-call(s32[40]{0:T(128)S(1)} %reshape.228.shift_ref, bf16[120,120]{1,0:T(8,128)(2,1)S(1)} %reshape.229.mix_ref, bf16[8,64,1920]{2,1,0:T(8,128)(2,1)S(1)} %bitcast.34, bf16[8,256,64]{2,1,0:T(8,128)(2,1)S(1)} %bitcast.35, bf16[64,64,256]{2,1,0:T(8,128)(2,1)S(1)} %bitcast.37), custom_call_target="tpu_custom_call" | custom-call | flops 3774873600 | bytes 6000000 | tf_op jit(solution)/shard_map/pallas_call | solution.py:197
  85.1 2.5 collective-permute-start
  87.6 0.5 compare_select_fusion.1
  88.1 0.6 pad_add_fusion.pair_ref
  88.8 0.6 pad_add_fusion.1.arrived_ref
  89.4 0.5 compare_convert_fusion.self_ref
  90.0 0.9 and_convert_fusion.mask_ref
  90.9 1.8 broadcast_select_fusion
  92.7 5.4 %reshape.232 = bf16[8,2,32,30,64]{4,3,2,1,0:T(8,128)(2,1)} reshape(bf16[8,64,1920]{2,1,0:T(8,128)(2,1)S(1)} %broadcast_select_fusion) | data formatting | bytes 3932160 | tf_op jit(solution)/shard_map/reshape | solution.py:223
  98.1 8.2 %copy.45 = bf16[8,30,32,2,64]{4,3,2,1,0:T(2,128)(2,1)} copy(bf16[8,30,32,2,64]{4,1,2,3,0:T(8,128)(2,1)} %bitcast.38) | data formatting | bytes 3932160 | tf_op jit(solution)/shard_map/reshape | solution.py:224
  106.2 5.1 %reshape.254.right_ref = bf16[8,30,4096]{2,1,0:T(8,128)(2,1)S(1)} reshape(bf16[8,30,32,2,64]{4,3,2,1,0:T(2,128)(2,1)} %copy.45) | data formatting | bytes 3932160 | tf_op jit(solution)/shard_map/reshape | solution.py:224
  111.4 36.5 %shard_map.123.gate_ref = bf16[40,256,1536]{2,1,0:T(8,128)(2,1)} custom-call(bf16[4,120,30]{2,1,0:T(8,128)(2,1)S(1)} %bitcast.36, bf16[8,30,4096]{2,1,0:T(8,128)(2,1)S(1)} %reshape.254.right_ref), custom_call_target="tpu_custom_call" | custom-call | flops 943718400 | bytes 36000000 | tf_op jit(solution)/shard_map/pallas_call | solution.py:227
  147.9 1.7 bitcast_select_fusion.left_ref
  149.6 132.1 %shard_map.124 = (f32[8,64,256]{2,1,0:T(8,128)}, f32[8,128]{1,0:T(8,128)}) custom-call(s32[80]{0:T(128)} %pad_add_fusion.pair_ref, s32[35]{0:T(128)} %min.10.slot_ref, s32[40]{0:T(128)} %compare_convert_fusion.self_ref, s32[80]{0:T(128)} %pad_add_fusion.1.arrived_ref, s32[40]{0:T(128)} %get-tuple-element.28.own_ref, f32[8,64,256]{2,1,0:T(8,128)} %and_convert_fusion.mask_ref, ...), custom_call_target="tpu_custom_call" | custom-call | tf_op jit(solution)/shard_map/pallas_call | solution.py:486
  281.7 1.2 slice.7
  282.9 1.9 copy.56
  (37 shorter events, 1.0 us)
Async XLA Ops:
  7.2 4.1 %copy-start = (s32[64,4]{0,1:T(4,128)S(1)}, s32[64,4]{0,1:T(4,128)}, u32[]{:S(2)}) copy-start(s32[64,4]{0,1:T(4,128)} %param.20) | copy-start | bytes 3076
  7.2 55.1 %all-gather.3.cloned.1.call-start = ((), (), s32[]{:S(2)}) async-start(), calls=%async_computation | async-start | bytes 2359296 | tf_op jit(solution)/shard_map/all_gather | solution.py:191
  7.9 83.0 %collective-permute-start.1 = (bf16[8,64,1920]{2,1,0:T(8,128)(2,1)}, bf16[8,64,1920]{2,1,0:T(8,128)(2,1)}, u32[]{:S(2)}, u32[]{:S(2)}) collective-permute-start(bf16[8,64,1920]{2,1,0:T(8,128)(2,1)} %bitcast.40), channel_id=1, source_target_pairs={{8,0},{16,8},{24,16},{9,1},{17,9},{25,17},{10,2},{18,10},{26,18},{... | collective-permute-start | bytes 5898248 | tf_op jit(solution)/shard_map/ppermute | solution.py:25
  29.4 10.2 %copy-start.2 = (bf16[1,8,64,1920]{3,2,1,0:T(8,128)(2,1)S(1)}, bf16[1,8,64,1920]{3,2,1,0:T(8,128)(2,1)}, u32[]{:S(2)}) copy-start(bf16[1,8,64,1920]{3,2,1,0:T(8,128)(2,1)} %param.11) | copy-start | bytes 5898244
  62.2 1.6 copy-start.3
  63.8 27.1 %copy-start.5 = (bf16[1,8,64,1920]{3,2,1,0:T(8,128)(2,1)S(1)}, bf16[1,8,64,1920]{3,2,1,0:T(8,128)(2,1)}, u32[]{:S(2)}) copy-start(bf16[1,8,64,1920]{3,2,1,0:T(8,128)(2,1)} %param.12) | copy-start | bytes 5898244
  85.1 62.8 %collective-permute-start = (bf16[40,64,384]{2,1,0:T(8,128)(2,1)}, bf16[40,64,384]{2,1,0:T(8,128)(2,1)}, u32[]{:S(2)}, u32[]{:S(2)}) collective-permute-start(bf16[40,64,384]{2,1,0:T(8,128)(2,1)} %shard_map.122), channel_id=1, source_target_pairs={{0,8},{8,16},{16,24},{1,9},{9,17},{17,25},{2,10},{10,18},{18,26},{... | collective-permute-start | bytes 5898248 | tf_op jit(solution)/shard_map/ppermute | solution.py:25
  111.4 36.5 %copy-start.4 = (bf16[8,5,64,384]{3,2,1,0:T(8,128)(2,1)S(1)}, bf16[8,5,64,384]{3,2,1,0:T(8,128)(2,1)}, u32[]{:S(2)}) copy-start(bf16[8,5,64,384]{3,2,1,0:T(8,128)(2,1)} %copy.38) | copy-start | bytes 5898244
  149.6 135.1 %copy-start.1 = (s32[64,4]{0,1:T(4,128)S(1)}, s32[64,4]{0,1:T(4,128)}, u32[]{:S(2)}) copy-start(s32[64,4]{0,1:T(4,128)} %param.20) | copy-start | bytes 3076
Sparse Core Ops, SparseCore 0:
  10.1 52.0 all-gather.2

commit v2 on v1

--- a/solution.py
+++ b/solution.py
@@ -34,14 +34,15 @@
     return joined_live.astype(jnp.float32).reshape(SEC_DEV, B, D * B)
 
 
+def step_at(place, group_total):
+    return group_total // 2 + (1 - 2 * (place % 2)) * ((place + 1) // 2)
+
+
 def send_order(group_total):
-    return sorted(range(1, group_total), key=lambda step: -min(step, group_total - step))
-
-
-def pair_tables(sector_shift, group, group_total):
-    target_list = lax.dynamic_slice_in_dim(sector_shift, group * SEC_DEV, SEC_DEV, 1).T.reshape(
-        SEC_DEV * CLASSES
-    )
+    return [step_at(place, group_total) for place in range(group_total - 1)]
+
+
+def pair_tables(target_list, group, group_total):
     steps = send_order(group_total)
     place_of = [group_total - 1] * group_total
     for place, step in enumerate(steps):
@@ -63,9 +64,10 @@
 def routing_tables(sector_shift, my_group, group_total, capacity):
     pairs = SEC_DEV * CLASSES
     groups = jnp.arange(group_total, dtype=jnp.int32)
+    target_lists = sector_shift.reshape(CLASSES, group_total, SEC_DEV).transpose(1, 2, 0)
     targets, places, positions, starts, ranks = jax.vmap(
-        lambda group: pair_tables(sector_shift, group, group_total)
-    )(groups)
+        lambda target_list, group: pair_tables(target_list, group, group_total)
+    )(target_lists.reshape(group_total, pairs), groups)
     mine = groups == my_group
     my_position = jnp.sum(jnp.where(mine[:, None], positions, 0), axis=0)
     my_start = jnp.sum(jnp.where(mine[:, None], starts, 0), axis=0)
@@ -90,25 +92,43 @@
     return sorted_pair, slot_source, from_self, arrived_slot, own_position
 
 
-def gate_kernel(mix_ref, right_ref, gate_ref, spread):
-    sites, channel_sites, _ = mix_ref.shape
+def gate_kernel(mix_ref, right_ref, *refs):
+    gate_ref, turned, low, spread = refs[-4:]
+    sites, channel_sites, depth = mix_ref.shape
     classes = gate_ref.shape[0]
-    halves = right_ref.shape[2] // 128
-    bond = 2 * halves
+    bond = right_ref.shape[1]
+    halves = bond // 2
+    channels = right_ref.shape[2] // bond
     per_class = channel_sites // classes
     low_lanes = lax.broadcasted_iota(jnp.int32, (halves, 128), 1) < 64
+    for channel in range(channels, depth):
+        turned[pl.ds(channel, halves, stride=depth), :] = jnp.zeros((halves, 128), jnp.float32)
+    for pair in range(channels // 2):
+        slab = right_ref[0, :, pair * 128 : (pair + 1) * 128].astype(jnp.float32)
+        one, two = slab[:halves], slab[halves:]
+        turned[pl.ds(2 * pair, halves, stride=depth), :] = jnp.where(
+            low_lanes, one, pltpu.roll(two, 64, 1)
+        )
+        turned[pl.ds(2 * pair + 1, halves, stride=depth), :] = jnp.where(
+            low_lanes, pltpu.roll(one, 64, 1), two
+        )
+    for half in range(halves):
+        low[:, half * 128 : (half + 1) * 128] = turned[half * depth : (half + 1) * depth, :].astype(
+            jnp.bfloat16
+        )
     for site in range(sites):
-        mixed = jnp.dot(mix_ref[site], right_ref[0], preferred_element_type=jnp.float32)
-        for half in range(halves):
-            spread[half * channel_sites : (half + 1) * channel_sites, :] = mixed[
-                :, half * 128 : (half + 1) * 128
-            ]
+        for half in range(0, halves, 2):
+            mixed = jnp.dot(
+                mix_ref[site], low[:, half * 128 : (half + 2) * 128], preferred_element_type=jnp.float32
+            )
+            spread[site % 2, half * channel_sites : (half + 1) * channel_sites, :] = mixed[:, :128]
+            spread[site % 2, (half + 1) * channel_sites : (half + 2) * channel_sites, :] = mixed[:, 128:]
 
         def one_class(charge, carry):
             for pair in range(per_class // 2):
                 first = charge * per_class + 2 * pair
-                one = spread[pl.ds(first, halves, stride=channel_sites), :]
-                two = spread[pl.ds(first + 1, halves, stride=channel_sites), :]
+                one = spread[site % 2, pl.ds(first, halves, stride=channel_sites), :]
+                two = spread[site % 2, pl.ds(first + 1, halves, stride=channel_sites), :]
                 upper = jnp.where(low_lanes, one, pltpu.roll(two, 64, 1))
                 lower = jnp.where(low_lanes, pltpu.roll(one, 64, 1), two)
                 lanes = slice(pair * 128, (pair + 1) * 128)
@@ -187,14 +207,15 @@
             ).astype(jnp.bfloat16)
 
 
-def build_environment(environment, site_blocks, channel_mix, sector_shift, offset):
+def build_environment(environment, site_blocks, channel_mix, sector_shift, offset, gate):
     every_site = lax.all_gather(site_blocks, "sec", axis=0, tiled=True)
+    every_site, gate = lax.optimization_barrier((every_site, gate))
     sectors = environment.shape[0]
     targets = lax.dynamic_slice_in_dim(sector_shift, offset, sectors, 1).reshape(-1)
     mix = channel_mix.transpose(2, 3, 0, 1).reshape(W * D, W * D)
     own = site_blocks.reshape(sectors, B, D, B).transpose(0, 2, 1, 3).reshape(sectors, D * B, B)
     per_columns = W // CLASSES * B
-    return pl.pallas_call(
+    fresh = pl.pallas_call(
         environment_kernel,
         grid=(sectors,),
         in_specs=[
@@ -215,30 +236,40 @@
             flops=8 * sectors * W * D * W * D * B * B, bytes_accessed=6000000, transcendentals=0
         ),
     )(targets, mix, environment, own, every_site)
-
-
-def build_gate(right_used, channel_mix):
+    return fresh, gate
+
+
+def build_gate(right_used, channel_mix, begin, end, gate):
     sectors = right_used.shape[0]
     halves = B // 2
-    right_split = right_used.reshape(sectors, 2, halves, W, B).transpose(0, 3, 2, 1, 4)
-    right_split = right_split.reshape(sectors, W, B * B)
+    depth = (W + 15) // 16 * 16
     mix = channel_mix.transpose(3, 0, 1, 2).reshape(D, W * D, W)
+    mix = jnp.pad(mix, ((0, 0), (0, 0), (0, depth - W)))
     shape = (sectors * CLASSES, D * B, W // CLASSES * D * B)
+    earlier = () if gate is None else (gate,)
     return pl.pallas_call(
         gate_kernel,
-        grid=(sectors,),
+        grid=(end - begin,),
         in_specs=[
-            pl.BlockSpec((D, W * D, W), lambda sector: (0, 0, 0)),
-            pl.BlockSpec((1, W, B * B), lambda sector: (sector, 0, 0)),
+            pl.BlockSpec(mix.shape, lambda sector: (0, 0, 0)),
+            pl.BlockSpec((1, B, W * B), lambda sector: (sector + begin, 0, 0)),
+        ]
+        + [pl.BlockSpec(memory_space=pl.ANY)] * len(earlier),
+        out_specs=pl.BlockSpec((CLASSES,) + shape[1:], lambda sector: (sector + begin, 0, 0)),
+        out_shape=jax.ShapeDtypeStruct(shape, jnp.bfloat16),
+        input_output_aliases={2: 0} if earlier else {},
+        scratch_shapes=[
+            pltpu.VMEM((halves * depth, 2 * B), jnp.float32),
+            pltpu.VMEM((depth, B * B), jnp.bfloat16),
+            pltpu.VMEM((2, halves * W * D, 2 * B), jnp.float32),
         ],
-        out_specs=pl.BlockSpec((CLASSES,) + shape[1:], lambda sector: (sector, 0, 0)),
-        out_shape=jax.ShapeDtypeStruct(shape, jnp.bfloat16),
-        scratch_shapes=[pltpu.VMEM((halves * W * D, 2 * B), jnp.float32)],
         compiler_params=pltpu.CompilerParams(vmem_limit_bytes=32 * 1024 * 1024),
         cost_estimate=pl.CostEstimate(
-            flops=2 * sectors * D * W * D * W * B * B, bytes_accessed=36000000, transcendentals=0
+            flops=16 * (end - begin) * D * W * D * W * B * B,
+            bytes_accessed=8000000 * (end - begin),
+            transcendentals=0,
         ),
-    )(mix, right_split)
+    )(mix, right_used, *earlier)
 
 
 def davidson_kernel(
@@ -329,44 +360,53 @@
         return [whole[entry : entry + 1, :] for entry in range(count)]
 
     def operator(turn, result):
-        def one_pair(position, carry):
+        def one_pair(position, slot):
             pair = pair_ref[position]
             sector = pair_ref[pairs + position]
             mixed = jnp.dot(low[sector], gate_ref[pair], preferred_element_type=jnp.float32)
             for channel in range(channels):
-                stacked[channel * rows : (channel + 1) * rows, :] = mixed[
+                stacked[slot, channel * rows : (channel + 1) * rows, :] = mixed[
                     :, channel * columns : (channel + 1) * columns
                 ].astype(jnp.bfloat16)
             partial[position] = jnp.dot(
-                left_ref[pair], stacked[...], preferred_element_type=jnp.float32
+                left_ref[pair], stacked[slot], preferred_element_type=jnp.float32
             )
-            return carry
-
-        copies = []
-        done = 0
-        for place, step in enumerate(steps):
-            upto = min((place + 1) * capacity, pairs)
-            lax.fori_loop(done, upto, one_pair, 0)
-            done = upto
+
+        def copy_at(place):
+            return pltpu.make_async_remote_copy(
+                src_ref=outgoing.at[turn, place],
+                dst_ref=incoming.at[turn, place],
+                send_sem=send_sem.at[turn, place],
+                recv_sem=recv_sem.at[turn, place],
+                device_id={"sec": lax.rem(me + step_at(place, n), n)},
+                device_id_type=pl.DeviceIdType.MESH,
+            )
+
+        def send(place):
             for rank in range(capacity):
                 outgoing[turn, place, rank] = partial[slot_ref[place * capacity + rank]].astype(
                     jnp.bfloat16
                 )
-            copies.append(
-                pltpu.make_async_remote_copy(
-                    src_ref=outgoing.at[turn, place],
-                    dst_ref=incoming.at[turn, place],
-                    send_sem=send_sem.at[turn, place],
-                    recv_sem=recv_sem.at[turn, place],
-                    device_id={"sec": lax.rem(me + step, n)},
-                    device_id_type=pl.DeviceIdType.MESH,
-                )
-            )
-            copies[-1].start()
-        if done < pairs:
-            lax.fori_loop(done, pairs, one_pair, 0)
-        for copy in copies:
-            copy.wait()
+            copy_at(place).start()
+
+        def one_place(place, carry):
+            for rank in range(capacity):
+                one_pair(place * capacity + rank, rank)
+            send(place)
+            return carry
+
+        whole_places = min(pairs // capacity, n - 1)
+        lax.fori_loop(0, whole_places, one_place, 0)
+        for position in range(whole_places * capacity, pairs):
+            one_pair(position, position % capacity)
+        for place in range(whole_places, n - 1):
+            send(place)
+
+        def wait_for(place, carry):
+            copy_at(place).wait()
+            return carry
+
+        lax.fori_loop(0, n - 1, wait_for, 0)
         landed = incoming.at[turn]
 
         def gather(sector, carry):
@@ -497,7 +537,7 @@
             vector,
             vector,
             pltpu.VMEM((sectors, rows, columns), jnp.bfloat16),
-            pltpu.VMEM((left_pairs.shape[2], columns), jnp.bfloat16),
+            pltpu.VMEM((capacity, left_pairs.shape[2], columns), jnp.bfloat16),
             pltpu.VMEM((pairs, rows, columns), jnp.float32),
             pltpu.VMEM((turns, others, capacity, rows, columns), jnp.bfloat16),
             pltpu.VMEM((turns, others, capacity, rows, columns), jnp.bfloat16),
@@ -547,7 +587,10 @@
     position = lax.axis_index("seg")
     came_right = passed_along(right_environment[0], "seg", -1)
     right_used = jnp.where(position == lax.axis_size("seg") - 1, right_environment[0], came_right)
-    fresh = build_environment(own_left, site_previous[0], channel_mix, sector_shift, offset)
+    gate = build_gate(right_used, channel_mix, 0, SEC_DEV // 2, None)
+    fresh, gate = build_environment(
+        own_left, site_previous[0], channel_mix, sector_shift, offset, gate
+    )
     handed = passed_along(fresh, "seg", 1)
     own_pairs = (
         own_left.reshape(SEC_DEV, B, CLASSES, W // CLASSES * B)
@@ -555,7 +598,7 @@
         .reshape(SEC_DEV * CLASSES, B, W // CLASSES * B)
     )
     left_pairs = jnp.where(position == 0, own_pairs, handed)
-    gate = build_gate(right_used, channel_mix)
+    gate = build_gate(right_used, channel_mix, SEC_DEV // 2, SEC_DEV, gate)
     tables = routing_tables(sector_shift, my_group, group_total, capacity)
     state, energy = davidson(
         tables, live_mask, state_start[0], preconditioner[0], left_pairs, gate, group_total, capacity

time: 293 us -> 265 us (0.904)
  local copies, waits for them, and re-layouts: 56.1 us -> 21.9 us
  waiting for transfers between devices: 16.3 us -> 20.1 us
  Pallas kernels: 190 us -> 193 us
    reshape x4 -> x2, local copies, waits for them, and re-layouts: 18.8 us -> 0.85 us  [the longest x1 0.78 us: routing_tables(): sector_shift.reshape(CLASSES, group_total, SEC_DEV).transpose(1, 2, 0)]
    gather x24 -> x0, local copies, waits for them, and re-layouts: 16 us -> none
    pallas_call x1 -> x2, Pallas kernels: 36.5 us -> 41.2 us  [build_gate(): pl.pallas_call(gate_kernel, grid=(end - begin,), in_specs=[pl.BlockSpec(m...]
    all_gather x1, waiting for transfers between devices: 15.6 us -> 19.4 us  [build_environment(): every_site = lax.all_gather(site_blocks, 'sec', axis=0, tiled=True)]
  transfers between devices with their start and end apart: 3 -> 3, of which waited for: 1 -> 1; matrix products, arithmetic and copies ran while one was open for 21% -> 9% of each run, Pallas kernels for 20% -> 16%
where the time goes in v2:
time: 265 us
  Pallas kernels  193 us (73%)
  local copies, waits for them, and re-layouts  21.9 us (8%)
  waiting for transfers between devices  20.1 us (8%)
  between operations  14.2 us (5%)
  other arithmetic  11.2 us (4%)
  starting transfers between devices  3.91 us (1%)
    pallas_call x1, Pallas kernels, davidson(): pl.pallas_call(kernel, out_shape=(jax.ShapeDtypeStruct(start.shape, jnp.f...  131 us
    pallas_call x2, Pallas kernels, build_gate(): pl.pallas_call(gate_kernel, grid=(end - begin,), in_specs=[pl.BlockSpec(m...  41.2 us
    pallas_call x1, Pallas kernels, build_environment(): pl.pallas_call(environment_kernel, grid=(sectors,), in_specs=[pl.BlockSpe...  21.2 us
    all_gather x1, waiting for transfers between devices, build_environment(): every_site = lax.all_gather(site_blocks, 'sec', axis=0, tiled=True)  19.4 us
    another operation x1, local copies, waits for them, and re-layouts, on_device(): own_left.reshape(SEC_DEV, B, CLASSES, W // CLASSES * B)  5.52 us
  transfers between devices with their start and end apart: 3, of which 1 were waited for; matrix products, arithmetic and copies ran while one was open for 9% of the time, Pallas kernels for 16%

profile of v2, /device:TPU:0, one launch (start us, length us, event | category | flops | bytes accessed | tf_op | source)
XLA Modules:
  0.0 264.5 jit_solution(2693195952607838058)
XLA Ops:
  7.2 0.0 copy-start
  7.2 0.0 all-gather.3.cloned.1.call-start
  7.2 0.7 all-gather.3.cloned.1.call-update
  7.9 1.3 collective-permute-start
  9.2 0.7 convert_element_type.27
  9.9 0.8 copy.39
  10.7 0.1 reshape.208
  10.8 0.8 constant_dynamic-slice_fusion.1
  11.6 1.0 multiply_bitcast_fusion
  12.6 1.2 reshape_squeeze.7
  13.8 0.0 copy-start.3
  13.8 0.1 reshape.211.shift_ref
  14.0 0.1 copy.36
  14.1 1.9 copy.35
  16.0 1.7 reshape.212.mix_ref
  17.7 0.0 copy-done.3
  17.7 0.1 select_reduce_fusion.1
  17.8 0.2 convert_reduce_fusion.2
  18.0 0.5 convert_reduce_fusion
  18.5 0.1 add_select_fusion.2
  18.6 0.1 select_reduce_fusion.2
  18.7 0.1 select_reduce_fusion.3
  18.8 0.8 select_reduce_fusion
  19.6 0.1 add_minimum_fusion
  19.7 0.0 collective-permute-done
  19.7 2.5 broadcast_select_fusion.right_ref
  22.2 20.6 %shard_map.122.refs_0_ = bf16[40,256,1536]{2,1,0:T(8,128)(2,1)} custom-call(bf16[4,120,32]{2,1,0:T(8,128)(2,1)S(1)} %pad.5.mix_ref, bf16[8,64,1920]{2,1,0:T(8,128)(2,1)S(1)} %broadcast_select_fusion.right_ref), custom_call_target="tpu_custom_call" | custom-call | flops 3774873600 | bytes 32000000 | tf_op jit(solution)/shard_map/pallas_call | solution.py:250
  42.8 19.4 %all-gather.3.cloned.1.call-done = bf16[1,64,64,256]{3,2,0,1:T(8,128)(2,1)} async-done(((bf16[1,8,64,256]{3,2,0,1:T(8,128)(2,1)}), bf16[1,64,64,256]{3,2,0,1:T(8,128)(2,1)}) %all-gather.3.cloned.1.call-update) | async-done | bytes 2097168 | tf_op jit(solution)/shard_map/all_gather | solution.py:211
  62.2 0.0 copy-start.1
  62.2 1.5 copy-done.1
  63.8 0.0 copy-start.2
  63.8 1.6 copy-done.2
  65.3 21.2 %shard_map.123 = bf16[40,64,384]{2,1,0:T(8,128)(2,1)} custom-call(s32[40]{0:T(128)S(1)} %reshape.211.shift_ref, bf16[120,120]{1,0:T(8,128)(2,1)S(1)} %reshape.212.mix_ref, bf16[8,64,1920]{2,1,0:T(8,128)(2,1)S(1)} %bitcast.28, bf16[8,256,64]{2,1,0:T(8,128)(2,1)S(1)} %bitcast.29, bf16[64,64,256]{2,1,0:T(8,128)(2,1)S(1)} %bitcast.30), custom_call_target="tpu_custom_call" | custom-call | flops 3774873600 | bytes 6000000 | tf_op jit(solution)/shard_map/pallas_call | solution.py:218
  86.6 2.6 collective-permute-start.1
  89.2 0.0 copy-done
  89.2 0.1 constant_dynamic-slice_fusion
  89.2 0.0 copy-start.4
  89.2 5.5 %reshape_squeeze.6 = bf16[8,64,5,384]{3,2,1,0:T(8,128)(2,1)} reshape(bf16[1,8,64,1920]{3,2,1,0:T(8,128)(2,1)} %param.11) | data formatting | bytes 3932160 | tf_op jit(solution)/shard_map/reshape;squeeze | solution.py:596
  94.8 0.0 copy-done.4
  94.8 0.1 dynamic_slice.9
  94.8 0.1 copy.33
  94.9 0.1 lt.114
  95.0 0.1 lt.116
  95.1 0.1 lt.117
  95.2 0.6 min.10.slot_ref
  95.8 0.1 reshape.209
  95.8 2.3 copy.34
  98.2 0.6 pad_add_fusion.pair_ref
  98.7 0.5 compare_select_fusion
  99.3 0.6 pad_add_fusion.1.arrived_ref
  99.9 0.6 compare_convert_fusion.self_ref
  100.4 0.1 iota_compare_fusion.4
  100.5 0.9 and_convert_fusion.mask_ref
  101.4 20.6 %shard_map.124.gate_ref = bf16[40,256,1536]{2,1,0:T(8,128)(2,1)} custom-call(bf16[4,120,32]{2,1,0:T(8,128)(2,1)S(1)} %pad.5.mix_ref, bf16[8,64,1920]{2,1,0:T(8,128)(2,1)S(1)} %broadcast_select_fusion.right_ref, bf16[40,256,1536]{2,1,0:T(8,128)(2,1)} %shard_map.122.refs_0_), custom_call_target="tpu_custom_call", output_to_operand_aliasing={{}: (2, {})} | custom-call | flops 3774873600 | bytes 32000000 | tf_op jit(solution)/shard_map/pallas_call | solution.py:250
  122.0 0.0 collective-permute-done.1
  122.0 1.7 bitcast_select_fusion.left_ref
  123.7 130.9 %shard_map.125 = (f32[8,64,256]{2,1,0:T(8,128)}, f32[8,128]{1,0:T(8,128)}) custom-call(s32[80]{0:T(128)} %pad_add_fusion.pair_ref, s32[35]{0:T(128)} %min.10.slot_ref, s32[40]{0:T(128)} %compare_convert_fusion.self_ref, s32[80]{0:T(128)} %pad_add_fusion.1.arrived_ref, s32[40]{0:T(128)} %get-tuple-element.16.own_ref, f32[8,64,256]{2,1,0:T(8,128)} %and_convert_fusion.mask_ref, ...), custom_call_target="tpu_custom_call" | custom-call | tf_op jit(solution)/shard_map/pallas_call | solution.py:526
  254.6 1.2 slice.7
  255.8 1.9 copy.42
  (11 shorter events, 0.2 us)
Async XLA Ops:
  7.2 82.0 %copy-start = (s32[64,4]{0,1:T(4,128)S(1)}, s32[64,4]{0,1:T(4,128)}, u32[]{:S(2)}) copy-start(s32[64,4]{0,1:T(4,128)} %param.20) | copy-start | bytes 3076
  7.2 55.0 %all-gather.3.cloned.1.call-start = ((), (), s32[]{:S(2)}) async-start(), calls=%async_computation | async-start | bytes 2359296 | tf_op jit(solution)/shard_map/all_gather | solution.py:211
  7.9 11.8 %collective-permute-start = (bf16[8,64,1920]{2,1,0:T(8,128)(2,1)}, bf16[8,64,1920]{2,1,0:T(8,128)(2,1)}, u32[]{:S(2)}, u32[]{:S(2)}) collective-permute-start(bf16[8,64,1920]{2,1,0:T(8,128)(2,1)} %bitcast.32), channel_id=1, source_target_pairs={{8,0},{16,8},{24,16},{9,1},{17,9},{25,17},{10,2},{18,10},{26,18},{... | collective-permute-start | bytes 5898248 | tf_op jit(solution)/shard_map/ppermute | solution.py:25
  13.8 3.9 %copy-start.3 = (s32[8]{0:T(128)S(1)}, s32[8]{0:T(128)}, u32[]{:S(2)}) copy-start(s32[8]{0:T(128)} %constant.79.clone) | copy-start | bytes 100
  62.2 1.5 copy-start.1
  63.8 1.6 copy-start.2
  86.6 35.5 %collective-permute-start.1 = (bf16[40,64,384]{2,1,0:T(8,128)(2,1)}, bf16[40,64,384]{2,1,0:T(8,128)(2,1)}, u32[]{:S(2)}, u32[]{:S(2)}) collective-permute-start(bf16[40,64,384]{2,1,0:T(8,128)(2,1)} %shard_map.123), channel_id=1, source_target_pairs={{0,8},{8,16},{16,24},{1,9},{9,17},{17,25},{2,10},{10,18},{18,26},{... | collective-permute-start | bytes 5898248 | tf_op jit(solution)/shard_map/ppermute | solution.py:25
  89.2 5.5 %copy-start.4 = (s32[64]{0:T(128)S(1)}, s32[64]{0:T(128)}, u32[]{:S(2)}) copy-start(s32[64]{0:T(128)} %param.19) | copy-start | bytes 772
Sparse Core Ops, SparseCore 0:
  10.1 52.0 all-gather.2

commit v3 on v2

--- a/solution.py
+++ b/solution.py
@@ -94,9 +94,11 @@
 
 def gate_kernel(mix_ref, right_ref, *refs):
     gate_ref, turned, low, spread = refs[-4:]
-    sites, channel_sites, depth = mix_ref.shape
+    depth = mix_ref.shape[1]
     classes = gate_ref.shape[0]
     bond = right_ref.shape[1]
+    sites = gate_ref.shape[1] // bond
+    channel_sites = mix_ref.shape[0] // sites
     halves = bond // 2
     channels = right_ref.shape[2] // bond
     per_class = channel_sites // classes
@@ -116,19 +118,21 @@
         low[:, half * 128 : (half + 1) * 128] = turned[half * depth : (half + 1) * depth, :].astype(
             jnp.bfloat16
         )
-    for site in range(sites):
-        for half in range(0, halves, 2):
-            mixed = jnp.dot(
-                mix_ref[site], low[:, half * 128 : (half + 2) * 128], preferred_element_type=jnp.float32
-            )
-            spread[site % 2, half * channel_sites : (half + 1) * channel_sites, :] = mixed[:, :128]
-            spread[site % 2, (half + 1) * channel_sites : (half + 2) * channel_sites, :] = mixed[:, 128:]
-
-        def one_class(charge, carry):
+    for half in range(0, halves, 2):
+        mixed = jnp.dot(
+            mix_ref[...], low[:, half * 128 : (half + 2) * 128], preferred_element_type=jnp.float32
+        )
+        for site in range(sites):
+            rows = slice(site * channel_sites, (site + 1) * channel_sites)
+            spread[site, half * channel_sites : (half + 1) * channel_sites, :] = mixed[rows, :128]
+            spread[site, (half + 1) * channel_sites : (half + 2) * channel_sites, :] = mixed[rows, 128:]
+
+    def one_class(charge, carry):
+        for site in range(sites):
             for pair in range(per_class // 2):
                 first = charge * per_class + 2 * pair
-                one = spread[site % 2, pl.ds(first, halves, stride=channel_sites), :]
-                two = spread[site % 2, pl.ds(first + 1, halves, stride=channel_sites), :]
+                one = spread[site, pl.ds(first, halves, stride=channel_sites), :]
+                two = spread[site, pl.ds(first + 1, halves, stride=channel_sites), :]
                 upper = jnp.where(low_lanes, one, pltpu.roll(two, 64, 1))
                 lower = jnp.where(low_lanes, pltpu.roll(one, 64, 1), two)
                 lanes = slice(pair * 128, (pair + 1) * 128)
@@ -136,12 +140,12 @@
                 gate_ref[charge, site * bond + halves : (site + 1) * bond, lanes] = lower.astype(
                     jnp.bfloat16
                 )
-            return carry
-
-        lax.fori_loop(0, classes, one_class, 0)
-
-
-def environment_kernel(shift_ref, mix_ref, left_ref, site_ref, every_ref, out_ref, spread, turned):
+        return carry
+
+    lax.fori_loop(0, classes, one_class, 0)
+
+
+def environment_kernel(shift_ref, mix_ref, left_ref, site_ref, every_ref, out_ref, own_ref, spread, turned):
     classes, bond, per_columns = out_ref.shape
     per_class = per_columns // bond
     mixed_rows = mix_ref.shape[0]
@@ -152,6 +156,7 @@
     sectors = pl.num_programs(0)
     low_lanes = lax.broadcasted_iota(jnp.int32, (halves, 128), 1) < 64
     for charge in range(classes):
+        own_ref[charge] = left_ref[0, :, charge * per_columns : (charge + 1) * per_columns]
         shifted = every_ref[shift_ref[charge * sectors + sector]]
         joined = lax.dot_general(
             shifted,
@@ -215,7 +220,9 @@
     mix = channel_mix.transpose(2, 3, 0, 1).reshape(W * D, W * D)
     own = site_blocks.reshape(sectors, B, D, B).transpose(0, 2, 1, 3).reshape(sectors, D * B, B)
     per_columns = W // CLASSES * B
-    fresh = pl.pallas_call(
+    pairs = pl.BlockSpec((CLASSES, B, per_columns), lambda sector: (sector, 0, 0))
+    shape = jax.ShapeDtypeStruct((sectors * CLASSES, B, per_columns), jnp.bfloat16)
+    fresh, own_pairs = pl.pallas_call(
         environment_kernel,
         grid=(sectors,),
         in_specs=[
@@ -225,8 +232,8 @@
             pl.BlockSpec((1, D * B, B), lambda sector: (sector, 0, 0)),
             pl.BlockSpec(every_site.shape, lambda sector: (0, 0, 0)),
         ],
-        out_specs=pl.BlockSpec((CLASSES, B, per_columns), lambda sector: (sector, 0, 0)),
-        out_shape=jax.ShapeDtypeStruct((sectors * CLASSES, B, per_columns), jnp.bfloat16),
+        out_specs=(pairs, pairs),
+        out_shape=(shape, shape),
         scratch_shapes=[
             pltpu.VMEM((B // 2 * W * D, 2 * B), jnp.float32),
             pltpu.VMEM((W * B, D * B), jnp.bfloat16),
@@ -236,22 +243,22 @@
             flops=8 * sectors * W * D * W * D * B * B, bytes_accessed=6000000, transcendentals=0
         ),
     )(targets, mix, environment, own, every_site)
-    return fresh, gate
+    return fresh, own_pairs, gate
 
 
 def build_gate(right_used, channel_mix, begin, end, gate):
     sectors = right_used.shape[0]
     halves = B // 2
     depth = (W + 15) // 16 * 16
-    mix = channel_mix.transpose(3, 0, 1, 2).reshape(D, W * D, W)
-    mix = jnp.pad(mix, ((0, 0), (0, 0), (0, depth - W)))
+    mix = channel_mix.transpose(3, 0, 1, 2).reshape(D * W * D, W)
+    mix = jnp.pad(mix, ((0, 0), (0, depth - W)))
     shape = (sectors * CLASSES, D * B, W // CLASSES * D * B)
     earlier = () if gate is None else (gate,)
     return pl.pallas_call(
         gate_kernel,
         grid=(end - begin,),
         in_specs=[
-            pl.BlockSpec(mix.shape, lambda sector: (0, 0, 0)),
+            pl.BlockSpec(mix.shape, lambda sector: (0, 0)),
             pl.BlockSpec((1, B, W * B), lambda sector: (sector + begin, 0, 0)),
         ]
         + [pl.BlockSpec(memory_space=pl.ANY)] * len(earlier),
@@ -261,7 +268,7 @@
         scratch_shapes=[
             pltpu.VMEM((halves * depth, 2 * B), jnp.float32),
             pltpu.VMEM((depth, B * B), jnp.bfloat16),
-            pltpu.VMEM((2, halves * W * D, 2 * B), jnp.float32),
+            pltpu.VMEM((D, halves * W * D, 2 * B), jnp.float32),
         ],
         compiler_params=pltpu.CompilerParams(vmem_limit_bytes=32 * 1024 * 1024),
         cost_estimate=pl.CostEstimate(
@@ -285,7 +292,7 @@
     start_ref,
     precondition_ref,
     left_ref,
-    gate_ref,
+    gate_source,
     state_ref,
     energy_ref,
     current,
@@ -303,6 +310,8 @@
     recv_sem,
     row_send_sem,
     row_recv_sem,
+    gate_ref,
+    gate_sem,
 ):
     pairs = left_ref.shape[0]
     sectors, rows, columns = current.shape
@@ -310,6 +319,13 @@
     channels = left_ref.shape[2] // rows
     steps = send_order(n)
     me = lax.axis_index("sec")
+    gate_copies = []
+    for sector in range(sectors):
+        part = pl.ds(sector * classes, classes)
+        gate_copies.append(
+            pltpu.make_async_copy(gate_source.at[part], gate_ref.at[part], gate_sem.at[sector])
+        )
+        gate_copies[-1].start()
 
     barrier = pltpu.get_barrier_semaphore()
     for step in steps:
@@ -438,6 +454,8 @@
         return carry
 
     lax.fori_loop(0, sectors, normalise, 0)
+    for copy in gate_copies:
+        copy.wait()
     operator(0, applied)
     energy = None
     for iteration in range(ITERS):
@@ -529,7 +547,7 @@
             jax.ShapeDtypeStruct(start.shape, jnp.float32),
             jax.ShapeDtypeStruct((8, 128), jnp.float32),
         ),
-        in_specs=[smem] * 5 + [vmem] * 5,
+        in_specs=[smem] * 5 + [vmem] * 4 + [pl.BlockSpec(memory_space=pl.ANY)],
         out_specs=(vmem, vmem),
         scratch_shapes=[
             vector,
@@ -547,6 +565,8 @@
             pltpu.SemaphoreType.DMA((turns, others)),
             pltpu.SemaphoreType.DMA((rounds, others)),
             pltpu.SemaphoreType.DMA((rounds, others)),
+            pltpu.VMEM(gate.shape, gate.dtype),
+            pltpu.SemaphoreType.DMA((sectors,)),
         ],
         compiler_params=pltpu.CompilerParams(
             collective_id=0, has_side_effects=True, vmem_limit_bytes=58 * 1024 * 1024
@@ -588,15 +608,10 @@
     came_right = passed_along(right_environment[0], "seg", -1)
     right_used = jnp.where(position == lax.axis_size("seg") - 1, right_environment[0], came_right)
     gate = build_gate(right_used, channel_mix, 0, SEC_DEV // 2, None)
-    fresh, gate = build_environment(
+    fresh, own_pairs, gate = build_environment(
         own_left, site_previous[0], channel_mix, sector_shift, offset, gate
     )
     handed = passed_along(fresh, "seg", 1)
-    own_pairs = (
-        own_left.reshape(SEC_DEV, B, CLASSES, W // CLASSES * B)
-        .transpose(0, 2, 1, 3)
-        .reshape(SEC_DEV * CLASSES, B, W // CLASSES * B)
-    )
     left_pairs = jnp.where(position == 0, own_pairs, handed)
     gate = build_gate(right_used, channel_mix, SEC_DEV // 2, SEC_DEV, gate)
     tables = routing_tables(sector_shift, my_group, group_total, capacity)

time: 265 us -> 249 us (0.940)
  Pallas kernels: 193 us -> 179 us
  local copies, waits for them, and re-layouts: 21.9 us -> 15.4 us
  waiting for transfers between devices: 20.1 us -> 24.3 us
    pallas_call x2, Pallas kernels: 41.2 us -> 32.9 us  [build_gate(): pl.pallas_call(gate_kernel, grid=(end - begin,), in_specs=[pl.BlockSpec(m...]
    another operation x1 -> x0, local copies, waits for them, and re-layouts: 5.52 us -> none  [on_device(): own_left.reshape(SEC_DEV, B, CLASSES, W // CLASSES * B)]
    pallas_call x1, Pallas kernels: 131 us -> 125 us  [davidson(): pl.pallas_call(kernel, out_shape=(jax.ShapeDtypeStruct(start.shape, jnp.f...]
    all_gather x1, waiting for transfers between devices: 19.4 us -> 23.6 us  [build_environment(): every_site = lax.all_gather(site_blocks, 'sec', axis=0, tiled=True)]
    unnamed x11 -> x15, local copies, waits for them, and re-layouts: 5.02 us -> 6.29 us
  transfers between devices with their start and end apart: 3 -> 3, of which waited for: 1 -> 1; matrix products, arithmetic and copies ran while one was open for 9% -> 7% of each run, Pallas kernels for 16% -> 13%
where the time goes in v3:
time: 249 us; the launch traced here: 248 us
  Pallas kernels  179 us (72%)
  waiting for transfers between devices  24.3 us (10%)
  local copies, waits for them, and re-layouts  15.4 us (6%)
  between operations  14.2 us (6%)
  other arithmetic  11.1 us (4%)
  starting transfers between devices  3.89 us (2%)
    pallas_call x1, Pallas kernels, davidson(): pl.pallas_call(kernel, out_shape=(jax.ShapeDtypeStruct(start.shape, jnp.f...  125 us
    pallas_call x2, Pallas kernels, build_gate(): pl.pallas_call(gate_kernel, grid=(end - begin,), in_specs=[pl.BlockSpec(m...  32.9 us
    all_gather x1, waiting for transfers between devices, build_environment(): every_site = lax.all_gather(site_blocks, 'sec', axis=0, tiled=True)  23.6 us
    pallas_call x1, Pallas kernels, build_environment(): pl.pallas_call(environment_kernel, grid=(sectors,), in_specs=[pl.BlockSpe...  21.1 us
    unnamed x15, local copies, waits for them, and re-layouts  6.29 us
  transfers between devices with their start and end apart: 3, of which 1 were waited for; matrix products, arithmetic and copies ran while one was open for 7% of the time, Pallas kernels for 13%

profile of v3, /device:TPU:0, one launch (start us, length us, event | category | flops | bytes accessed | tf_op | source)
XLA Modules:
  0.0 248.2 jit_solution(17274933908462711364)
XLA Ops:
  7.2 0.0 copy-start
  7.2 0.0 all-gather.3.cloned.1.call-start
  7.2 0.7 all-gather.3.cloned.1.call-update
  7.9 1.3 collective-permute-start
  9.2 0.7 convert_element_type.27
  9.9 0.8 copy.35
  10.7 0.1 reshape.205
  10.8 0.8 constant_dynamic-slice_fusion.1
  11.6 1.0 multiply_bitcast_fusion
  12.6 1.2 reshape_squeeze.3
  13.8 0.0 copy-start.5
  13.8 0.1 reshape.207.shift_ref
  14.0 0.1 copy.32
  14.1 1.9 copy.31
  16.0 1.7 reshape.208.mix_ref
  17.7 0.0 copy-done.5
  17.7 0.1 select_reduce_fusion.1
  17.8 0.2 convert_reduce_fusion.2
  18.0 0.5 convert_reduce_fusion
  18.5 0.1 add_select_fusion.2
  18.6 0.1 select_reduce_fusion.2
  18.7 0.1 select_reduce_fusion.3
  18.8 0.8 select_reduce_fusion
  19.6 0.1 add_minimum_fusion
  19.7 0.0 collective-permute-done
  19.7 2.5 broadcast_select_fusion.right_ref
  22.2 16.5 %shard_map.122.refs_0_ = bf16[40,256,1536]{2,1,0:T(8,128)(2,1)} custom-call(bf16[480,32]{1,0:T(8,128)(2,1)S(1)} %pad.5.mix_ref, bf16[8,64,1920]{2,1,0:T(8,128)(2,1)S(1)} %broadcast_select_fusion.right_ref), custom_call_target="tpu_custom_call" | custom-call | flops 3774873600 | bytes 32000000 | tf_op jit(solution)/shard_map/pallas_call | solution.py:257
  38.7 23.6 %all-gather.3.cloned.1.call-done = bf16[1,64,64,256]{3,2,0,1:T(8,128)(2,1)} async-done(((bf16[1,8,64,256]{3,2,0,1:T(8,128)(2,1)}), bf16[1,64,64,256]{3,2,0,1:T(8,128)(2,1)}) %all-gather.3.cloned.1.call-update) | async-done | bytes 2097168 | tf_op jit(solution)/shard_map/all_gather | solution.py:216
  62.2 0.0 copy-start.3
  62.2 1.6 copy-done.3
  63.8 0.0 copy-start.4
  63.8 1.5 copy-done.4
  65.4 0.0 copy-start.6
  65.4 21.1 %shard_map.123 = (bf16[40,64,384]{2,1,0:T(8,128)(2,1)}, bf16[40,64,384]{2,1,0:T(8,128)(2,1)S(1)}) custom-call(s32[40]{0:T(128)S(1)} %reshape.207.shift_ref, bf16[120,120]{1,0:T(8,128)(2,1)S(1)} %reshape.208.mix_ref, bf16[8,64,1920]{2,1,0:T(8,128)(2,1)S(1)} %bitcast.25, bf16[8,256,64]{2,1,0:T(8,128)(2,1)S(1)} %bitcast.23, bf16[64,64,256]{2,1,0:T(8,128)(2,1)S(1)} %bitcast.24), custom_call_target="tpu_custom_call" | custom-call | flops 3774873600 | bytes 6000000 | tf_op jit(solution)/shard_map/pallas_call | solution.py:225
  86.5 0.0 copy-start.1
  86.5 1.3 copy-done.1
  87.8 2.6 %collective-permute-start.1 = (bf16[40,64,384]{2,1,0:T(8,128)(2,1)}, bf16[40,64,384]{2,1,0:T(8,128)(2,1)}, u32[]{:S(2)}, u32[]{:S(2)}) collective-permute-start(bf16[40,64,384]{2,1,0:T(8,128)(2,1)} %get-tuple-element.10), channel_id=1, source_target_pairs={{0,8},{8,16},{16,24},{1,9},{9,17},{17,25},{2,10},{10,18},{18,26},{... | collective-permute-start | bytes 5898248 | tf_op jit(solution)/shard_map/ppermute | solution.py:25
  90.3 0.0 copy-done
  90.3 0.1 constant_dynamic-slice_fusion
  90.4 0.0 copy-done.6
  90.4 0.1 dynamic_slice.9
  90.5 0.1 copy.30
  90.6 0.1 lt.114
  90.7 0.1 lt.116
  90.7 0.1 lt.117
  90.8 0.7 min.10.slot_ref
  91.5 0.1 reshape.206
  91.6 0.6 pad_add_fusion.pair_ref
  92.2 0.5 compare_select_fusion
  92.7 0.6 pad_add_fusion.1.arrived_ref
  93.3 0.6 compare_convert_fusion.self_ref
  93.8 0.1 iota_compare_fusion.4
  93.9 0.9 and_convert_fusion.mask_ref
  94.9 0.0 copy-start.2
  94.9 16.5 %shard_map.124.gate_source = bf16[40,256,1536]{2,1,0:T(8,128)(2,1)} custom-call(bf16[480,32]{1,0:T(8,128)(2,1)S(1)} %pad.5.mix_ref, bf16[8,64,1920]{2,1,0:T(8,128)(2,1)S(1)} %broadcast_select_fusion.right_ref, bf16[40,256,1536]{2,1,0:T(8,128)(2,1)} %shard_map.122.refs_0_), custom_call_target="tpu_custom_call", output_to_operand_aliasing={{}: (2, {})} | custom-call | flops 3774873600 | bytes 32000000 | tf_op jit(solution)/shard_map/pallas_call | solution.py:257
  111.3 0.0 collective-permute-done.1
  111.3 0.0 copy-done.2
  111.3 1.6 broadcast_select_fusion.1.left_ref
  112.9 125.4 %shard_map.125 = (f32[8,64,256]{2,1,0:T(8,128)}, f32[8,128]{1,0:T(8,128)}) custom-call(s32[80]{0:T(128)} %pad_add_fusion.pair_ref, s32[35]{0:T(128)} %min.10.slot_ref, s32[40]{0:T(128)} %compare_convert_fusion.self_ref, s32[80]{0:T(128)} %pad_add_fusion.1.arrived_ref, s32[40]{0:T(128)} %get-tuple-element.20.own_ref, f32[8,64,256]{2,1,0:T(8,128)} %and_convert_fusion.mask_ref, ...), custom_call_target="tpu_custom_call" | custom-call | tf_op jit(solution)/shard_map/pallas_call | solution.py:544
  238.3 1.2 slice.7
  239.5 1.9 copy.38
  (11 shorter events, 0.2 us)
Async XLA Ops:
  7.2 83.2 %copy-start = (s32[64,4]{0,1:T(4,128)S(1)}, s32[64,4]{0,1:T(4,128)}, u32[]{:S(2)}) copy-start(s32[64,4]{0,1:T(4,128)} %param.20) | copy-start | bytes 3076
  7.2 55.1 %all-gather.3.cloned.1.call-start = ((), (), s32[]{:S(2)}) async-start(), calls=%async_computation | async-start | bytes 2359296 | tf_op jit(solution)/shard_map/all_gather | solution.py:216
  7.9 11.8 %collective-permute-start = (bf16[8,64,1920]{2,1,0:T(8,128)(2,1)}, bf16[8,64,1920]{2,1,0:T(8,128)(2,1)}, u32[]{:S(2)}, u32[]{:S(2)}) collective-permute-start(bf16[8,64,1920]{2,1,0:T(8,128)(2,1)} %bitcast.26), channel_id=1, source_target_pairs={{8,0},{16,8},{24,16},{9,1},{17,9},{25,17},{10,2},{18,10},{26,18},{... | collective-permute-start | bytes 5898248 | tf_op jit(solution)/shard_map/ppermute | solution.py:25
  13.8 3.9 %copy-start.5 = (s32[8]{0:T(128)S(1)}, s32[8]{0:T(128)}, u32[]{:S(2)}) copy-start(s32[8]{0:T(128)} %constant.79.clone) | copy-start | bytes 100
  62.2 1.6 copy-start.3
  63.8 1.5 copy-start.4
  65.4 25.0 %copy-start.6 = (s32[64]{0:T(128)S(1)}, s32[64]{0:T(128)}, u32[]{:S(2)}) copy-start(s32[64]{0:T(128)} %param.19) | copy-start | bytes 772
  86.5 1.3 copy-start.1
  87.8 23.6 %collective-permute-start.1 = (bf16[40,64,384]{2,1,0:T(8,128)(2,1)}, bf16[40,64,384]{2,1,0:T(8,128)(2,1)}, u32[]{:S(2)}, u32[]{:S(2)}) collective-permute-start(bf16[40,64,384]{2,1,0:T(8,128)(2,1)} %get-tuple-element.10), channel_id=1, source_target_pairs={{0,8},{8,16},{16,24},{1,9},{9,17},{17,25},{2,10},{10,18},{18,26},{... | collective-permute-start | bytes 5898248 | tf_op jit(solution)/shard_map/ppermute | solution.py:25
  94.9 16.5 %copy-start.2 = (bf16[40,64,384]{2,1,0:T(8,128)(2,1)S(1)}, bf16[40,64,384]{2,1,0:T(8,128)(2,1)}, u32[]{:S(2)}) copy-start(bf16[40,64,384]{2,1,0:T(8,128)(2,1)} %copy-done.1) | copy-start | bytes 5898244
Sparse Core Ops, SparseCore 0:
  10.1 52.0 all-gather.2
